TPU v7x, 128 devices: a whole 4x4x4 slice. The times are simulated.
128 devices in a mesh: dp: 8 (over z, x_hi), mp: 16 (over x_lo, y, core).
Axes of the slice: x: 4 (x_hi: 2, x_lo: 2; x = x_hi * 2 + x_lo), y: 4, z: 4, core: 2. Of those that a mesh axis runs over, the one named last changes fastest.
Arguments:
- hidden_in: bfloat16 [16384, 8192], P('dp', 'mp'), may hold values from -6 to 6
- positions: int32 [16384], P('dp'), may hold values from 0 to 127, as said below
- assignment: int32 [8, 16], P('dp'), may hold values from 0 to 15, each once within a row
- query_weight: bfloat16 [8192, 8192], P(None, 'mp'), may hold values from -0.0625 to 0.0625
- kv_weight: bfloat16 [8192, 2048], P(None, 'mp'), may hold values from -0.0625 to 0.0625
- dt_weight: float32 [8192, 64], replicated, may hold values from -0.0625 to 0.0625
- dt_bias: float32 [64], replicated, may hold values from -3 to -1
- decay_log: float32 [64], replicated, may hold values from -5.3 to -0.7
- skip_gain: float32 [64], replicated, may hold values from 0.5 to 1.5
Outputs:
- student_out: bfloat16 [16384, 8192], P(('dp', 'mp'))
- grad_dt_weight: float32 [8192, 64], replicated
- grad_dt_bias: float32 [64], replicated
- grad_decay_log: float32 [64], replicated
- grad_skip_gain: float32 [64], replicated
- loss: float32 [], replicated
Inputs may be any that keep to these rules, and one draw needn't show every extreme that they name: `assignment`: row g lists each of the 16 sequences of group g once. positions count up by one from 0 at each document start; every sequence of 128 rows begins a document, and the first sequence is one whole document.
All inputs are finite; a program needn't handle non-finite values.
Results may differ from a plain program's by a relative error of at most 0.0065.
Values may be sent and summed in bfloat16 or wider, within the bound.
A program may use at most 128 MiB of HBM per device.

v0:
```python
import jax
import jax.numpy as jnp
from jax import lax
from jax.sharding import PartitionSpec as P

QH = 64
KVH = 8
HD = 128


highest = lax.Precision.HIGHEST


def from_partner(shard, axis, stride):
    return lax.ppermute(shard, axis, [(i, i ^ 1 << stride) for i in range(lax.axis_size(axis))])


def rotate(values, spots):
    half = HD // 2
    frequency = 500000.0 ** (-jnp.arange(half, dtype=jnp.float32) * 2.0 / HD)
    angle = spots.astype(jnp.float32)[:, None] * frequency[None, :]
    cosine = jnp.cos(angle)[:, None, :]
    sine = jnp.sin(angle)[:, None, :]
    first = values[..., :half].astype(jnp.float32)
    second = values[..., half:].astype(jnp.float32)
    turned = jnp.concatenate(
        [first * cosine - second * sine, second * cosine + first * sine], axis=-1
    )
    return turned.astype(jnp.bfloat16)


def join_pair(mine, other, member, bit_index):
    upper = member // (1 << bit_index) % 2
    return jnp.where(
        upper == 0, jnp.concatenate([mine, other], 1), jnp.concatenate([other, mine], 1)
    )


def attend(query, head_pair, spots, seq_len):
    count = query.shape[0]
    heads = query.shape[1] // HD
    seqs = count // seq_len
    query_turned = rotate(query.reshape(count, heads, HD), spots).reshape(seqs, seq_len, heads, HD)
    key_turned = rotate(head_pair[:, :HD].reshape(count, 1, HD), spots).reshape(seqs, seq_len, HD)
    values = head_pair[:, HD:].reshape(seqs, seq_len, HD)
    scores = jnp.einsum(
        "slhd,smd->shlm", query_turned, key_turned, preferred_element_type=jnp.float32
    ) * HD ** (-0.5)
    causal = jnp.tril(jnp.ones((seq_len, seq_len), bool))
    scores = jnp.where(causal, scores, -jnp.inf)
    biggest = jnp.max(scores, axis=-1, keepdims=True)
    weights = jnp.exp(scores - biggest)
    probabilities = (weights / jnp.sum(weights, axis=-1, keepdims=True)).astype(jnp.bfloat16)
    target = jnp.einsum("shlm,smd->slhd", probabilities, values, preferred_element_type=jnp.float32)
    return target.astype(jnp.bfloat16).reshape(count, heads * HD)


def student(dt_weight, dt_bias, decay_log, skip_gain, rows, query, key_value):
    seq_len = rows.shape[0]
    ratio = QH // KVH
    step_size = jax.nn.softplus(
        jnp.dot(rows.astype(jnp.float32), dt_weight, precision=highest) + dt_bias
    )
    level = jnp.cumsum(step_size * -jnp.exp(decay_log), axis=0)
    level = level.T.reshape(KVH, ratio, seq_len)
    widths = step_size.T.reshape(KVH, ratio, 1, seq_len)
    query_wide = query.astype(jnp.float32).reshape(seq_len, KVH, ratio, HD)
    pairs = key_value.astype(jnp.float32).reshape(seq_len, KVH, 2, HD)
    scores = jnp.einsum("tgjn,sgn->gjts", query_wide, pairs[:, :, 0], precision=highest) * HD ** (
        -0.5
    )
    causal = jnp.tril(jnp.ones((seq_len, seq_len), bool))
    spread = level[..., :, None] - level[..., None, :]
    decay = jnp.where(causal, jnp.exp(jnp.where(causal, spread, 0.0)), 0.0)
    mixed = jnp.einsum("gjts,sgn->tgjn", scores * decay * widths, pairs[:, :, 1], precision=highest)
    mixed = mixed + skip_gain.reshape(KVH, ratio)[None, :, :, None] * pairs[:, :, None, 1]
    return mixed.reshape(seq_len, QH * HD)


def local(
    hidden_in,
    positions,
    assignment,
    query_weight,
    kv_weight,
    dt_weight,
    dt_bias,
    decay_log,
    skip_gain,
):
    group_size = lax.axis_size("mp")
    member = lax.axis_index("mp")
    rows_total = hidden_in.shape[0]
    seq_len = rows_total // group_size
    order = assignment[0]
    piece = lax.all_gather(hidden_in, "mp", axis=1, tiled=True)
    query_part = jnp.dot(piece, query_weight, preferred_element_type=jnp.float32)
    pair_part = jnp.dot(piece, kv_weight, preferred_element_type=jnp.float32)
    query = query_part.astype(jnp.bfloat16)
    key_value = pair_part.astype(jnp.bfloat16)
    head_pair = key_value
    head_pair = join_pair(head_pair, from_partner(head_pair, "mp", 0), member, 0)
    target = attend(query, head_pair, positions, seq_len)

    def reorder(values):
        shaped = values.reshape(group_size, seq_len, values.shape[1])
        return jnp.take(shaped, order, axis=0).reshape(rows_total, values.shape[1])

    total = lax.axis_size("dp") * rows_total * QH * HD
    rows_own, query_own, pairs_own, target_own = (
        lax.all_to_all(reorder(hidden_in), "mp", split_axis=0, concat_axis=1, tiled=True),
        lax.all_to_all(reorder(query), "mp", split_axis=0, concat_axis=1, tiled=True),
        lax.all_to_all(reorder(key_value), "mp", split_axis=0, concat_axis=1, tiled=True),
        lax.all_to_all(reorder(target), "mp", split_axis=0, concat_axis=1, tiled=True),
    )

    def objective(weight_dt, bias_dt, log_decay, gain_skip):
        mixed = student(weight_dt, bias_dt, log_decay, gain_skip, rows_own, query_own, pairs_own)
        differ = mixed - target_own.astype(jnp.float32)
        return (jnp.sum(differ * differ) / total, mixed)

    partial_loss, pullback, mixed = jax.vjp(
        objective, dt_weight, dt_bias, decay_log, skip_gain, has_aux=True
    )
    grads = pullback(jnp.ones((), jnp.float32))
    mixed_out = mixed.astype(jnp.bfloat16)
    summed = lax.psum((grads[0], grads[1], grads[2], grads[3], partial_loss), ("dp", "mp"))
    return (mixed_out, summed[0], summed[1], summed[2], summed[3], summed[4])


def solution(mesh):
    placed = (
        P("dp", "mp"),
        P("dp"),
        P("dp", None),
        P(None, "mp"),
        P(None, "mp"),
        P(),
        P(),
        P(),
        P(),
    )
    return jax.shard_map(
        local,
        mesh=mesh,
        in_specs=placed,
        out_specs=(P(("dp", "mp"), None), P(), P(), P(), P(), P()),
        check_vma=False,
    )
```

profile of v0, /device:TPU:0, one launch (start us, length us, event | category | flops | bytes accessed | tf_op | source)
XLA Modules:
  0.0 524.0 jit_solution(11447401861205530174)
XLA Ops:
  9.3 3.6 gather_fusion.2
  12.9 169.8 %all-gather.2.cloned.1.call-done = bf16[2048,8192]{1,0:T(8,128)(2,1)} async-done(((bf16[2048,512]{1,0:T(8,128)(2,1)}), bf16[2048,8192]{1,0:T(8,128)(2,1)}) %all-gather.2.cloned.1.call-update) | async-done | bytes 33554448 | tf_op jit(solution)/shard_map/all_gather | solution.py:96
  182.8 15.9 %convolution_convert_fusion.1 = bf16[2048,128]{1,0:T(8,128)(2,1)} fusion(bf16[2048,8192]{1,0:T(8,128)(2,1)} %all-gather.2.cloned.1.call-done, bf16[8192,128]{1,0:T(8,128)(2,1)S(1)} %copy-done), kind=kOutput, calls=%fused_computation.32 | convolution fusion | flops 4295229440 | bytes 36175872 | tf_op jit(solution)/shard_map/dot_general | solution.py:98
  201.3 4.7 all-to-all-start
  206.0 23.8 %convolution_convert_fusion = bf16[2048,512]{1,0:T(8,128)(2,1)S(1)} fusion(bf16[2048,8192]{1,0:T(8,128)(2,1)} %all-gather.2.cloned.1.call-done, bf16[8192,512]{1,0:T(8,128)(2,1)} %param.14), kind=kOutput, calls=%fused_computation.27 | convolution fusion | flops 17180917760 | bytes 44040192 | tf_op jit(solution)/shard_map/dot_general | solution.py:97
  231.7 4.6 broadcast_select_fusion.1
  236.4 5.7 %all-to-all-start.2 = ((bf16[16,128,512]{2,1,0:T(8,128)(2,1)}), bf16[16,128,512]{2,1,0:T(8,128)(2,1)S(1)}, u32[]{:S(2)}, u32[]{:S(2)}) async-start(bf16[16,128,512]{2,1,0:T(8,128)(2,1)} %get-tuple-element.47), calls=%async_computation.2 | async-start | bytes 4194304 | tf_op jit(solution)/shard_map/all_to_all | solution.py:111
  245.4 3.9 copy.78
  260.0 10.9 %all-to-all-done.2 = bf16[16,128,512]{2,1,0:T(8,128)(2,1)S(1)} async-done(((bf16[16,128,512]{2,1,0:T(8,128)(2,1)}), bf16[16,128,512]{2,1,0:T(8,128)(2,1)S(1)}, u32[]{:S(2)}, u32[]{:S(2)}) %all-to-all-start.2) | async-done | bytes 2097184 | tf_op jit(solution)/shard_map/all_to_all | solution.py:111
  270.9 5.6 %all-to-all-start.1 = ((bf16[16,128,512]{2,1,0:T(8,128)(2,1)}), bf16[16,128,512]{2,1,0:T(8,128)(2,1)}, u32[]{:S(2)}, u32[]{:S(2)}) async-start(bf16[16,128,512]{2,1,0:T(8,128)(2,1)} %get-tuple-element.48), calls=%async_computation.1 | async-start | bytes 4194304 | tf_op jit(solution)/shard_map/all_to_all | solution.py:112
  276.5 4.9 fusion.38
  281.4 3.8 fusion.17
  292.5 12.8 %all-to-all-done.1 = bf16[16,128,512]{2,1,0:T(8,128)(2,1)} async-done(((bf16[16,128,512]{2,1,0:T(8,128)(2,1)}), bf16[16,128,512]{2,1,0:T(8,128)(2,1)}, u32[]{:S(2)}, u32[]{:S(2)}) %all-to-all-start.1) | async-done | bytes 2097184 | tf_op jit(solution)/shard_map/all_to_all | solution.py:112
  305.3 5.6 %all-to-all-start.3 = ((bf16[16,128,512]{1,2,0:T(8,128)(2,1)}), bf16[16,128,512]{1,2,0:T(8,128)(2,1)}, u32[]{:S(2)}, u32[]{:S(2)}) async-start(bf16[16,128,512]{1,2,0:T(8,128)(2,1)} %broadcast_select_fusion), calls=%async_computation.3 | async-start | bytes 4194304 | tf_op jit(solution)/shard_map/all_to_all | solution.py:114
  315.4 3.9 copy.48
  322.5 4.3 fusion.43
  326.8 12.9 %all-to-all-done.3 = bf16[16,128,512]{1,2,0:T(8,128)(2,1)} async-done(((bf16[16,128,512]{1,2,0:T(8,128)(2,1)}), bf16[16,128,512]{1,2,0:T(8,128)(2,1)}, u32[]{:S(2)}, u32[]{:S(2)}) %all-to-all-start.3) | async-done | bytes 2097184 | tf_op jit(solution)/shard_map/all_to_all | solution.py:114
  342.6 7.2 %multiply_reduce_fusion = (f32[]{:T(128)}, f32[8,8]{1,0:T(8,128)S(1)}, f32[128,8,8,128]{0,3,2,1:T(8,128)S(1)}, bf16[128,8,8,128]{0,3,2,1:T(8,128)(2,1)}) fusion(f32[128,8,128]{0,2,1:T(8,128)S(1)} %broadcast_multiply_fusion, f32[128,8,8,128]{0,3,2,1:T(8,128)S(1)} %bitcast.176, f32[128,8,128]{0,2,1:T(8,128)S(1)} %copy-done.7, f32[8,8]{1,0:T(8,128)S(1)} %mul.198, ...), kind=kOutput, calls=%fused_computation.14 | convolution fusion | flops 1626341376 | bytes 16109828 | tf_op jit(solution)/shard_map/jvp(gjts,sgn->tgjn)/dot_general | solution.py:75
  349.8 6.8 %fusion.65 = (f32[8,8,128]{2,1,0:T(8,128)S(1)}, f32[8,8,128]{2,1,0:T(8,128)S(1)}, f32[8,8,128]{2,1,0:T(8,128)S(1)}) fusion(f32[8,8,128]{2,1,0:T(8,128)S(1)} %bitcast.188, f32[8,8,128]{2,1,0:T(8,128)S(1)} %fusion.46, f32[8,128,128,8]{1,2,3,0:T(8,128)S(1)} %copy-done.4, pred[128,128]{1,0:T(8,128)(4,1)S(1)} %iota_compare_fusion, ...), kind=kOutput, calls=%fused_computation.118 | convolution fusion | flops 1627365376 | bytes 8863744 | tf_op jit(solution)/shard_map/transpose(jvp(gjts,sgn->tgjn))/dot_general | solution.py:75
  358.1 3.6 fusion.70
  361.8 4.2 copy.65
  366.7 68.6 %all-reduce = (f32[64]{0:T(128)}, f32[64]{0:T(128)}, f32[64]{0:T(128)}, f32[]{:T(128)}) all-reduce(f32[64]{0:T(128)S(1)} %get-tuple-element.35, f32[64]{0:T(128)S(1)} %negate_multiply_fusion, f32[64]{0:T(128)S(1)} %reshape.275, f32[]{:T(128)S(6)} %div.25), channel_id=1, replica_groups=mesh['dp'=8,'mp'=16] {'dp','mp'}, use_global_device_ids=true, to_apply=%region_9.11 | all-reduce | flops 193 | bytes 1544 | tf_op jit(solution)/shard_map/psum | solution.py:127
  435.3 78.8 %all-reduce.3.cloned.1.call-done = f32[8192,64]{0,1:T(8,128)} async-done(((f32[8192,64]{0,1:T(8,128)}), f32[8192,64]{0,1:T(8,128)}) %all-reduce.3.cloned.1.call-update) | async-done | bytes 2097168 | tf_op jit(solution)/shard_map/psum | solution.py:127
  514.1 3.1 copy.84
  (75 shorter events, 40.1 us)
Async XLA Ops:
  7.2 175.6 %copy-start = (bf16[8192,128]{1,0:T(8,128)(2,1)S(1)}, bf16[8192,128]{1,0:T(8,128)(2,1)}, u32[]{:S(2)}) copy-start(bf16[8192,128]{1,0:T(8,128)(2,1)} %param.15) | copy-start | bytes 6291460
  7.2 5.7 %copy-start.10 = (s32[1,16]{1,0:T(1,128)S(1)}, s32[1,16]{1,0:T(1,128)}, u32[]{:S(2)}) copy-start(s32[1,16]{1,0:T(1,128)} %param.13) | copy-start | bytes 196
  7.2 175.6 %all-gather.2.cloned.1.call-start = ((), (), s32[]{:S(2)}) async-start(), calls=%async_computation.4 | async-start | bytes 35651584 | tf_op jit(solution)/shard_map/all_gather | solution.py:96
  201.3 35.1 %all-to-all-start = ((bf16[16,128,128]{2,1,0:T(8,128)(2,1)}), bf16[16,128,128]{2,1,0:T(8,128)(2,1)S(1)}, u32[]{:S(2)}, u32[]{:S(2)}) async-start(bf16[16,128,128]{2,1,0:T(8,128)(2,1)} %broadcast_select_fusion.3), calls=%async_computation | async-start | bytes 1048576 | tf_op jit(solution)/shard_map/all_to_all | solution.py:113
  229.8 6.6 %copy-start.3 = (bf16[2048,512]{1,0:T(8,128)(2,1)}, bf16[2048,512]{1,0:T(8,128)(2,1)S(1)}, u32[]{:S(2)}) copy-start(bf16[2048,512]{1,0:T(8,128)(2,1)S(1)} %convolution_convert_fusion) | copy-start | bytes 6291460
  236.4 12.9 %copy-start.5 = (bf16[16,128,128]{2,1,0:T(8,128)(2,1)}, bf16[16,128,128]{2,1,0:T(8,128)(2,1)S(1)}, u32[]{:S(2)}) copy-start(bf16[16,128,128]{2,1,0:T(8,128)(2,1)S(1)} %all-to-all-done) | copy-start | bytes 1572868
  236.4 34.5 %all-to-all-start.2 = ((bf16[16,128,512]{2,1,0:T(8,128)(2,1)}), bf16[16,128,512]{2,1,0:T(8,128)(2,1)S(1)}, u32[]{:S(2)}, u32[]{:S(2)}) async-start(bf16[16,128,512]{2,1,0:T(8,128)(2,1)} %get-tuple-element.47), calls=%async_computation.2 | async-start | bytes 4194304 | tf_op jit(solution)/shard_map/all_to_all | solution.py:111
  245.0 13.1 %collective-permute-start = (bf16[2048,128]{1,0:T(8,128)(2,1)}, bf16[2048,128]{1,0:T(8,128)(2,1)}, u32[]{:S(2)}, u32[]{:S(2)}) collective-permute-start(bf16[2048,128]{1,0:T(8,128)(2,1)} %convolution_convert_fusion.1), channel_id=1, source_target_pairs={{0,1},{1,0},{2,3},{3,2},{4,5},{5,4},{6,7},{7,6},{8,9},{9,8},{10,11... | collective-permute-start | bytes 1572872 | tf_op jit(solution)/shard_map/ppermute | solution.py:15
  270.9 14.3 %copy-start.2 = (bf16[16,128,512]{2,1,0:T(8,128)(2,1)}, bf16[16,128,512]{2,1,0:T(8,128)(2,1)S(1)}, u32[]{:S(2)}) copy-start(bf16[16,128,512]{2,1,0:T(8,128)(2,1)S(1)} %all-to-all-done.2) | copy-start | bytes 6291460
  270.9 34.4 %all-to-all-start.1 = ((bf16[16,128,512]{2,1,0:T(8,128)(2,1)}), bf16[16,128,512]{2,1,0:T(8,128)(2,1)}, u32[]{:S(2)}, u32[]{:S(2)}) async-start(bf16[16,128,512]{2,1,0:T(8,128)(2,1)} %get-tuple-element.48), calls=%async_computation.1 | async-start | bytes 4194304 | tf_op jit(solution)/shard_map/all_to_all | solution.py:112
  290.9 20.2 %copy-start.9 = (f32[64]{0:T(128)S(1)}, f32[64]{0:T(128)}, u32[]{:S(2)}) copy-start(f32[64]{0:T(128)} %param.19) | copy-start | bytes 772
  290.9 20.3 %copy-start.11 = (f32[64]{0:T(128)S(1)}, f32[64]{0:T(128)}, u32[]{:S(2)}) copy-start(f32[64]{0:T(128)} %param.18) | copy-start | bytes 772
  290.9 20.3 %copy-start.6 = (bf16[16,128,128]{2,1,0:T(8,128)(2,1)S(1)}, bf16[16,128,128]{2,1,0:T(8,128)(2,1)}, u32[]{:S(2)}) copy-start(bf16[16,128,128]{2,1,0:T(8,128)(2,1)} %copy-done.5) | copy-start | bytes 1572868
  305.3 34.4 %all-to-all-start.3 = ((bf16[16,128,512]{1,2,0:T(8,128)(2,1)}), bf16[16,128,512]{1,2,0:T(8,128)(2,1)}, u32[]{:S(2)}, u32[]{:S(2)}) async-start(bf16[16,128,512]{1,2,0:T(8,128)(2,1)} %broadcast_select_fusion), calls=%async_computation.3 | async-start | bytes 4194304 | tf_op jit(solution)/shard_map/all_to_all | solution.py:114
  310.8 203.2 %all-reduce.3.cloned.1.call-start = ((), (), s32[]{:S(2)}) async-start(), calls=%async_computation.5 | async-start | bytes 4194304 | tf_op jit(solution)/shard_map/psum | solution.py:127
  312.4 7.0 %copy-start.8 = (f32[64]{0:T(128)S(1)}, f32[64]{0:T(128)}, u32[]{:S(2)}) copy-start(f32[64]{0:T(128)} %param.17) | copy-start | bytes 772
  339.7 2.8 copy-start.4
  339.7 2.9 copy-start.7
  361.8 155.3 %copy-start.1 = (bf16[8192,128]{1,0:T(8,128)(2,1)S(1)}, bf16[8192,128]{1,0:T(8,128)(2,1)}, u32[]{:S(2)}) copy-start(bf16[8192,128]{1,0:T(8,128)(2,1)} %param.15) | copy-start | bytes 6291460
Sparse Core Ops, SparseCore 0:
  9.7 173.0 all-gather.1
  361.8 152.1 all-reduce.2
where the time goes:
time: 526 us; the launch traced here: 524 us
  waiting for transfers between devices  286 us (54%)
  matrix products  70.2 us (13%)
  blocking collectives  68.6 us (13%)
  local copies, waits for them, and re-layouts  36 us (7%)
  other arithmetic  26.1 us (5%)
  starting transfers between devices  22.2 us (4%)
  between operations  15 us (3%)
    all_gather x1, waiting for transfers between devices, local(): piece = lax.all_gather(hidden_in, 'mp', axis=1, tiled=True)  170 us
    psum x1, waiting for transfers between devices, local(): lax.psum((grads[0], grads[1], grads[2], grads[3], partial_loss), ('dp', '...  78.8 us
    psum x1, blocking collectives, local(): lax.psum((grads[0], grads[1], grads[2], grads[3], partial_loss), ('dp', '...  68.6 us
    dot_general x1, matrix products, local(): jnp.dot(piece, query_weight, preferred_element_type=jnp.float32)  23.8 us
    dot_general x1, matrix products, local(): pair_part = jnp.dot(piece, kv_weight, preferred_element_type=jnp.float32)  15.9 us
    dot_general x2, matrix products, student(): jnp.einsum('gjts,sgn->tgjn', scores * decay * widths, pairs[:, :, 1], pre...  14 us
    all_to_all x1, waiting for transfers between devices, local(): lax.all_to_all(reorder(target), 'mp', split_axis=0, concat_axis=1, tiled=...  12.9 us
    all_to_all x1, waiting for transfers between devices, local(): lax.all_to_all(reorder(query), 'mp', split_axis=0, concat_axis=1, tiled=T...  12.8 us
  transfers between devices with their start and end apart: 7, of which 5 were waited for; matrix products, arithmetic and copies ran while one was open for 17% of the time, Pallas kernels for 0%

commit v1 on v0

v1 whole, which is shorter than its diff:
```python
import jax
import jax.numpy as jnp
from jax import lax
from jax.experimental import pallas as pl
from jax.experimental.pallas import tpu as pltpu
from jax.sharding import PartitionSpec as P

D = 8192
QH = 64
HD = 128
L = 128
RATIO = 8
CHUNKS = 8
CHIPS = 8
KB = 1024
TOTAL = 16384 * QH * HD
SCALE = HD**-0.5
KT = 384
NW = 1536
FAR = 4

highest = lax.Precision.HIGHEST
f32 = jnp.float32
bf16 = jnp.bfloat16


def dot_nt(a, b):
    return lax.dot_general(a, b, (((1,), (1,)), ((), ())), preferred_element_type=f32)


def dot_nn(a, b):
    return jnp.dot(a, b, preferred_element_type=f32)


def body(
    order,
    bias_s,
    decay_s,
    gain_s,
    positions,
    x_in,
    qw,
    kvw,
    dtw,
    out,
    gw_out,
    small_out,
    a_buf,
    w_buf,
    x_send,
    dt_stage,
    acc,
    qb,
    qt,
    s_t,
    s_s,
    n_buf,
    pb,
    o_buf,
    pre_t,
    gw,
    small,
    mixed,
    ex_ss,
    ex_rs,
    g_ss,
    g_rs,
    w_sem,
    wr_ss,
    wr_rs,
    o_ss,
    o_rs,
):
    me = lax.axis_index("mp")
    core = me % 2
    chip = me // 2
    x = chip // 4
    y = chip % 4
    xo = 1 - x
    up = (y + 1) % 4
    down = (y + 3) % 4
    across = (y + 2) % 4

    def device(xx, yy):
        return (xx * 4 + yy) * 2 + core

    partner = chip * 2 + (1 - core)
    to_up, to_down, to_x = device(x, up), device(x, down), device(xo, y)

    barrier = pltpu.get_barrier_semaphore()
    for step in range(1, 16):
        pl.semaphore_signal(barrier, inc=1, device_id={"mp": (me + step) % 16})
    pl.semaphore_wait(barrier, 15)

    q_cols = pl.ds(pl.multiple_of(core * 512, 512), 512)
    kv_cols = pl.ds(pl.multiple_of(1024 + core * 128, 128), 128)

    def remote(src, dst, ss, rs, dev):
        return pltpu.make_async_remote_copy(
            src_ref=src, dst_ref=dst, send_sem=ss, recv_sem=rs, device_id={"mp": dev}
        )

    def stage(i, carry):
        a_buf[i, chip, :, q_cols] = x_in[order[0, core * CHUNKS + i]]
        x_send[i] = x_in[order[0, (1 - core) * CHUNKS + i]]
        return carry

    lax.fori_loop(0, CHUNKS, stage, 0)

    def exchange(i):
        return remote(x_send.at[i], a_buf.at[i, chip, :, q_cols], ex_ss.at[i], ex_rs.at[i], partner)

    def start_exchange(i, carry):
        exchange(i).start()
        return carry

    lax.fori_loop(0, CHUNKS, start_exchange, 0)

    w_copies = (
        pltpu.make_async_copy(dtw, dt_stage, w_sem.at[2]),
        pltpu.make_async_copy(qw, w_buf.at[:, q_cols], w_sem.at[0]),
        pltpu.make_async_copy(kvw, w_buf.at[:, kv_cols], w_sem.at[1]),
    )
    w_remote = (
        remote(qw, w_buf.at[:, q_cols], wr_ss.at[0], wr_rs.at[0], partner),
        remote(kvw, w_buf.at[:, kv_cols], wr_ss.at[1], wr_rs.at[1], partner),
    )

    first = pl.ds(0, KT)
    second = pl.ds(KT, KB - KT)
    every = pl.ds(0, L)
    low = pl.ds(0, L // 2)
    high = pl.ds(L // 2, L // 2)
    whole = pl.ds(0, KB)

    def hop(kind, i):
        slot_x, slot_y, rows, cols, dev = (
            (x, y, every, whole, to_up),
            (x, y, every, whole, to_down),
            (x, y, every, whole, to_x),
            (x, down, low, first, to_up),
            (x, down, every, second, to_up),
            (x, down, every, first, to_x),
            (x, up, high, first, to_down),
            (x, up, every, first, to_x),
            (xo, y, every, second, to_up),
            (xo, y, every, second, to_down),
            (x, across, every, first, to_x),
            (xo, up, every, second, to_down),
        )[kind]
        ref = a_buf.at[i, slot_x * 4 + slot_y, rows, cols]
        return remote(ref, ref, g_ss.at[i, kind], g_rs.at[i, kind], dev)

    def hop1(i):
        exchange(i).wait_recv()
        for kind in (0, 1, 2):
            hop(kind, i).start()

    def hop2(i):
        hop(0, i).wait_recv()
        for kind in (4, 3, 5):
            hop(kind, i).start()
        hop(1, i).wait_recv()
        for kind in (6, 7):
            hop(kind, i).start()
        hop(2, i).wait_recv()
        for kind in (9, 8):
            hop(kind, i).start()

    def hop3(i):
        hop(9, i).wait_recv()
        hop(11, i).start()
        hop(3, i).wait_recv()
        hop(6, i).wait_recv()
        hop(10, i).start()

    def arrived(i):
        for kind in (4, 5, 7, 8, 10, 11):
            hop(kind, i).wait_recv()

    for i in range(FAR):
        hop1(i)
    for c in w_copies:
        c.start()
    for c in w_remote:
        c.start()

    w_copies[0].wait()

    def split_dt(r, carry):
        rows = pl.ds(pl.multiple_of(r * 512, 512), 512)
        w = dt_stage[rows, :]
        one = w.astype(bf16).astype(f32)
        left = w - one
        two = left.astype(bf16).astype(f32)
        three = left - two
        w_buf[rows, 1280:1408] = jnp.concatenate([one, two], axis=1).astype(bf16)
        w_buf[rows, 1408:1536] = jnp.concatenate([three, jnp.zeros_like(three)], axis=1).astype(bf16)
        return carry

    lax.fori_loop(0, D // 512, split_dt, 0)
    gw[...] = jnp.zeros_like(gw)
    small[...] = jnp.zeros_like(small)

    row_i = lax.broadcasted_iota(jnp.int32, (L, L), 0)
    col_i = lax.broadcasted_iota(jnp.int32, (L, L), 1)
    causal = col_i <= row_i
    upper = jnp.where(row_i <= col_i, 1.0, 0.0).astype(f32)
    lower = jnp.where(row_i >= col_i, 1.0, 0.0).astype(f32)
    head_row = lax.broadcasted_iota(jnp.int32, (RATIO, L), 0)

    def per_head(ref):
        values = jnp.zeros((RATIO, L), f32)
        for h in range(RATIO):
            values = jnp.where(head_row == h, ref[chip * RATIO + h], values)
        return values

    def out_copy(i):
        dst = out.at[:, pl.ds(pl.multiple_of(chip * KB, KB), KB)]
        target = core * CHUNKS + i

        def far():
            return remote(mixed.at[i], dst, o_ss.at[i], o_rs.at[chip], target)

        def near():
            return pltpu.make_async_copy(mixed.at[i], dst, o_rs.at[chip])

        return target, far, near

    def compute(i):
        def project(n, carry):
            cols = pl.ds(pl.multiple_of(n * 256, 256), 256)
            total = dot_nn(a_buf[i, 0], w_buf[0:KB, cols])
            for m in range(1, CHIPS):
                total += dot_nn(a_buf[i, m], w_buf[m * KB : (m + 1) * KB, cols])
            acc[:, cols] = total
            return carry

        lax.fori_loop(0, NW // 256, project, 0)

        spots = positions[pl.ds(order[0, core * CHUNKS + i], 1), :].astype(f32)
        spots = jnp.broadcast_to(spots, (L, L)).T
        lane = col_i % (HD // 2)
        frequency = jnp.exp(lane.astype(f32) * f32(-2.0 / HD * 13.122363377404328))
        angle = spots * frequency
        cosine = jnp.cos(angle)
        sine = jnp.where(col_i < HD // 2, -jnp.sin(angle), jnp.sin(angle))

        def rotate(head):
            wide = head.astype(f32)
            return (wide * cosine + pltpu.roll(wide, HD // 2, 1) * sine).astype(bf16)

        k = acc[:, 1024:1152].astype(bf16)
        v = acc[:, 1152:1280].astype(bf16)
        v32 = v.astype(f32)
        k_turned = rotate(k)
        for h in range(RATIO):
            rows = pl.ds(h * L, L)
            q = acc[:, h * HD : (h + 1) * HD].astype(bf16)
            qb[rows, :] = q
            qt[rows, :] = rotate(q)
        s_t[...] = dot_nt(qt[...], k_turned)
        s_s[...] = dot_nt(qb[...], k)
        for h in range(RATIO):
            rows = pl.ds(h * L, L)
            scores = jnp.where(causal, s_t[rows, :] * SCALE, -jnp.inf)
            weights = jnp.exp(scores - jnp.max(scores, axis=1, keepdims=True))
            pb[rows, :] = weights.astype(bf16)
        o_buf[...] = dot_nn(pb[...], jnp.concatenate([v, jnp.ones_like(v)], axis=1))

        pre = acc[:, 1280:1408] + acc[:, 1408:1536]
        pre = pre + pltpu.roll(pre, QH, 1)
        pre_t[...] = pre.T
        raw = pre_t[pl.ds(pl.multiple_of(chip * RATIO, RATIO), RATIO), :] + per_head(bias_s)
        step_size = jnp.maximum(raw, 0.0) + jnp.log1p(jnp.exp(-jnp.abs(raw)))
        rate = -jnp.exp(per_head(decay_s))
        summed = jnp.dot(step_size, upper, precision=highest, preferred_element_type=f32)
        level = rate * summed
        level_t = jnp.concatenate([level, jnp.zeros((L - RATIO, L), f32)], axis=0).T
        for h in range(RATIO):
            rows = pl.ds(h * L, L)
            spread = jnp.where(causal, level_t[:, h : h + 1] - level[h : h + 1, :], -jnp.inf)
            kept = s_s[rows, :] * SCALE * jnp.exp(spread)
            n_buf[rows, :] = kept
            pb[rows, :] = (kept * step_size[h : h + 1, :]).astype(bf16)
        s_s[...] = dot_nn(pb[...], v)
        gain_rows, loss_rows = [], []
        for h in range(RATIO):
            rows = pl.ds(h * L, L)
            teacher = o_buf[rows, :]
            target = (teacher[:, :HD] / teacher[:, HD:]).astype(bf16).astype(f32)
            value = s_s[rows, :] + gain_s[chip * RATIO + h] * v32
            mixed[i, :, h * HD : (h + 1) * HD] = value.astype(bf16)
            differ = value - target
            gain_rows.append(jnp.sum(differ * v32, axis=0, keepdims=True))
            loss_rows.append(jnp.sum(differ * differ, axis=0, keepdims=True))
            pb[rows, :] = differ.astype(bf16)
        target, far, near = out_copy(i)
        pl.when(target == me)(lambda: near().start())
        pl.when(target != me)(lambda: far().start())

        s_t[...] = dot_nt(pb[...], v)
        col_rows, row_cols = [], jnp.zeros((L, L), f32)
        for h in range(RATIO):
            rows = pl.ds(h * L, L)
            product = s_t[rows, :] * n_buf[rows, :]
            col_rows.append(jnp.sum(product, axis=0, keepdims=True))
            along = jnp.sum(product * step_size[h : h + 1, :], axis=1, keepdims=True)
            row_cols = jnp.where(col_i == h, along, row_cols)
        factor = f32(2.0 / TOTAL)
        by_col = jnp.concatenate(col_rows, axis=0) * factor
        by_row = row_cols.T[:RATIO, :] * factor
        d_level = by_row - step_size * by_col
        behind = jnp.dot(d_level, lower, precision=highest, preferred_element_type=f32)
        d_step = by_col + rate * behind
        d_raw = d_step * (1.0 / (1.0 + jnp.exp(-raw)))
        small[0:8, :] += d_raw
        small[8:16, :] += d_level * level
        small[16:24, :] += jnp.concatenate(gain_rows, axis=0) * factor
        small[24:32, :] += jnp.concatenate(loss_rows, axis=0) * f32(1.0 / TOTAL)
        upper_part = d_raw.astype(bf16).astype(f32)
        parts = jnp.concatenate([upper_part, d_raw - upper_part], axis=0).astype(bf16)
        for m in range(CHIPS):
            cols = slice(m * KB, (m + 1) * KB)
            gw[:, cols] += dot_nn(parts, a_buf[i, m])

    hop2(0)
    hop2(1)
    hop3(0)

    def phase(i, carry):
        pl.when(i + 1 < CHUNKS)(lambda: hop3(i + 1))
        pl.when(i + 2 < CHUNKS)(lambda: hop2(i + 2))
        pl.when(i + FAR < CHUNKS)(lambda: hop1(i + FAR))

        @pl.when(i == 0)
        def _():
            for c in w_copies[1:]:
                c.wait()
            for c in w_remote:
                c.wait_recv()

        arrived(i)
        compute(i)
        return carry

    lax.fori_loop(0, CHUNKS, phase, 0)

    gw_out[...] = gw[0:8, :] + gw[8:16, :]
    small_out[...] = small[...]

    def finish(i, carry):
        for kind in range(12):
            hop(kind, i).wait_send()
        exchange(i).wait_send()
        target, far, _ = out_copy(i)
        pl.when(target != me)(lambda: far().wait_send())
        dst = out.at[:, pl.ds(pl.multiple_of(i * KB, KB), KB)]
        pltpu.make_async_copy(mixed.at[i], dst, o_rs.at[i]).wait()
        return carry

    lax.fori_loop(0, CHUNKS, finish, 0)
    for c in w_remote:
        c.wait_send()


def fused(order, bias, decay, gain, positions, hidden, qw, kvw, dtw):
    smem = pl.BlockSpec(memory_space=pltpu.SMEM)
    vmem = pl.BlockSpec(memory_space=pltpu.VMEM)
    hbm = pl.BlockSpec(memory_space=pl.ANY)
    dma = pltpu.SemaphoreType.DMA
    stacked = (RATIO * L, HD)
    return pl.pallas_call(
        body,
        out_shape=(
            jax.ShapeDtypeStruct((L, D), bf16),
            jax.ShapeDtypeStruct((RATIO, D), f32),
            jax.ShapeDtypeStruct((32, L), f32),
        ),
        in_specs=[smem, smem, smem, smem, vmem, vmem, hbm, hbm, hbm],
        out_specs=(hbm, vmem, vmem),
        scratch_shapes=[
            pltpu.VMEM((CHUNKS, CHIPS, L, KB), bf16),
            pltpu.VMEM((D, NW), bf16),
            pltpu.VMEM((CHUNKS, L, 512), bf16),
            pltpu.VMEM((D, QH), f32),
            pltpu.VMEM((L, NW), f32),
            pltpu.VMEM(stacked, bf16),
            pltpu.VMEM(stacked, bf16),
            pltpu.VMEM(stacked, f32),
            pltpu.VMEM(stacked, f32),
            pltpu.VMEM(stacked, f32),
            pltpu.VMEM(stacked, bf16),
            pltpu.VMEM((RATIO * L, 2 * HD), f32),
            pltpu.VMEM((L, L), f32),
            pltpu.VMEM((16, D), f32),
            pltpu.VMEM((32, L), f32),
            pltpu.VMEM((CHUNKS, L, KB), bf16),
            dma((CHUNKS,)),
            dma((CHUNKS,)),
            dma((CHUNKS, 12)),
            dma((CHUNKS, 12)),
            dma((3,)),
            dma((2,)),
            dma((2,)),
            dma((CHUNKS,)),
            dma((CHIPS,)),
        ],
        name="fused",
        compiler_params=pltpu.CompilerParams(
            collective_id=0, has_side_effects=True, vmem_limit_bytes=60 * 2**20
        ),
    )(order, bias, decay, gain, positions, hidden, qw, kvw, dtw)


def local(
    hidden_in,
    positions,
    assignment,
    query_weight,
    kv_weight,
    dt_weight,
    dt_bias,
    decay_log,
    skip_gain,
):
    student_out, gw, small = fused(
        assignment,
        dt_bias,
        decay_log,
        skip_gain,
        positions.reshape(16, L),
        hidden_in.reshape(16, L, 512),
        query_weight,
        kv_weight,
        dt_weight,
    )
    sums = jnp.sum(small.reshape(4, RATIO, L), axis=2)
    gw, sums = lax.psum((gw, sums), "dp")
    gw = lax.all_gather(gw, "mp", axis=0)
    sums = lax.all_gather(sums, "mp", axis=0)
    gw = gw.reshape(CHIPS, 2, RATIO, D).sum(1).reshape(QH, D).T
    sums = sums.reshape(CHIPS, 2, 4, RATIO).sum(1).transpose(1, 0, 2).reshape(4, QH)
    return student_out, gw, sums[0], sums[1], sums[2], jnp.sum(sums[3])


def solution(mesh):
    placed = (
        P("dp", "mp"),
        P("dp"),
        P("dp", None),
        P(None, "mp"),
        P(None, "mp"),
        P(),
        P(),
        P(),
        P(),
    )
    return jax.shard_map(
        local,
        mesh=mesh,
        in_specs=placed,
        out_specs=(P(("dp", "mp"), None), P(), P(), P(), P(), P()),
        check_vma=False,
    )
```

time: 526 us -> 327 us (0.62)
  waiting for transfers between devices: 286 us -> 87.1 us
  Pallas kernels: 0 us -> 172 us
  matrix products: 70.2 us -> 0 us
  local copies, waits for them, and re-layouts: 36 us -> 6.95 us
  blocking collectives: 68.6 us -> 39.9 us
  starting transfers between devices: 22.2 us -> 0.08 us
  other arithmetic: 26.1 us -> 5.6 us
    pallas_call x0 -> x1, Pallas kernels: none -> 172 us  [fused(): pl.pallas_call(body, out_shape=(jax.ShapeDtypeStruct((L, D), bf16), jax.S...]
    all_gather x1, waiting for transfers between devices: 170 us -> 0.01 us  [local(): gw = lax.all_gather(gw, 'mp', axis=0)]
    dot_general x9 -> x0, matrix products: 70.2 us -> none  [the longest x1 23.8 us: local(): jnp.dot(piece, query_weight, preferred_element_type=jnp.float32)]
    psum x1, blocking collectives: 68.6 us -> 20.3 us  [local(): gw, sums = lax.psum((gw, sums), 'dp')]
    all_to_all x4 -> x0, waiting for transfers between devices: 36.5 us -> none  [the longest x1 12.9 us: local(): lax.all_to_all(reorder(target), 'mp', split_axis=0, concat_axis=1, tiled=...]
    all_to_all x4 -> x0, starting transfers between devices: 21.5 us -> none  [the longest x1 5.71 us: local(): lax.all_to_all(reorder(hidden_in), 'mp', split_axis=0, concat_axis=1, til...]
    all_gather x0 -> x1, blocking collectives: none -> 19.6 us  [local(): sums = lax.all_gather(sums, 'mp', axis=0)]
    gather x4 -> x0, local copies, waits for them, and re-layouts: 9.79 us -> none  [reorder(): return jnp.take(shaped, order, axis=0).reshape(rows_total, values.shape[1])]
  transfers between devices with their start and end apart: 7 -> 2, of which waited for: 5 -> 1; matrix products, arithmetic and copies ran while one was open for 17% -> 1% of each run, Pallas kernels for 0% -> 0%
where the time goes in v1:
time: 327 us; the launch traced here: 325 us
  Pallas kernels  172 us (53%)
  waiting for transfers between devices  87.1 us (27%)
  blocking collectives  39.9 us (12%)
  between operations  14.1 us (4%)
  local copies, waits for them, and re-layouts  6.95 us (2%)
  other arithmetic  5.6 us (2%)
    pallas_call x1, Pallas kernels, fused(): pl.pallas_call(body, out_shape=(jax.ShapeDtypeStruct((L, D), bf16), jax.S...  172 us
    psum x1, waiting for transfers between devices, local(): gw, sums = lax.psum((gw, sums), 'dp')  87.1 us
    psum x1, blocking collectives, local(): gw, sums = lax.psum((gw, sums), 'dp')  20.3 us
    all_gather x1, blocking collectives, local(): sums = lax.all_gather(sums, 'mp', axis=0)  19.6 us
  transfers between devices with their start and end apart: 2, of which 1 were waited for; matrix products, arithmetic and copies ran while one was open for 1% of the time, Pallas kernels for 0%

profile of v1, /device:TPU:0, one launch (start us, length us, event | category | flops | bytes accessed | tf_op | source)
XLA Modules:
  0.0 325.4 jit_solution(1550292650978260744)
XLA Ops:
  7.2 0.0 all-reduce.2.cloned.1.call-start
  7.2 3.8 %copy.16.dtw = f32[8192,64]{1,0:T(8,128)} copy(f32[8192,64]{0,1:T(8,128)} %param.14) | data formatting | bytes 4194304 | tf_op args[5]
  11.0 171.6 %fused.1 = (bf16[128,8192]{1,0:T(8,128)(2,1)}, f32[8,8192]{1,0:T(8,128)}, f32[32,128]{1,0:T(8,128)}) custom-call(s32[1,16]{1,0:T(1,128)} %order.1, f32[64]{0:T(128)} %bias_s.1, f32[64]{0:T(128)} %decay_s.1, f32[64]{0:T(128)} %gain_s.1, s32[16,128]{1,0:T(8,128)} %bitcast.15, bf16[16,128,512]{2,1,0:T(8,128)(2,1)} %bitcast.12, bf16[8192,512]{1,0:T(8,128)(2,1)} %qw.1, ...), custom_call_target="tpu_custom_call" | custom-call | tf_op jit(solution)/shard_map/fused/pallas_call | solution.py:373
  182.6 0.0 all-reduce.2.cloned.1.call-update
  182.6 0.0 all-gather.2.cloned.1.call-start
  182.7 87.1 %all-reduce.2.cloned.1.call-done = f32[1,8,8192]{2,1,0:T(8,128)} async-done(((f32[1,8,8192]{2,1,0:T(8,128)}), f32[1,8,8192]{2,1,0:T(8,128)}) %all-reduce.2.cloned.1.call-update) | async-done | bytes 262160 | tf_op jit(solution)/shard_map/psum | solution.py:439
  269.8 0.0 all-gather.2.cloned.1.call-update
  269.8 0.8 reduce_sum.39
  270.6 0.1 all_gather.14
  270.7 20.3 %psum.15 = f32[1,4,8]{2,1,0:T(4,128)S(1)} all-reduce(f32[1,4,8]{2,1,0:T(4,128)S(1)} %all_gather.14), channel_id=1, replica_groups=mesh['dp'=8,'mp'=16] {'dp'}, use_global_device_ids=true, to_apply=%region_3.0 | all-reduce | flops 32 | bytes 256 | tf_op jit(solution)/shard_map/psum | solution.py:439
  291.0 19.6 %all_gather.15 = f32[16,4,8]{2,1,0:T(4,128)S(1)} all-gather(f32[1,4,8]{2,1,0:T(4,128)S(1)} %psum.15), channel_id=1, replica_groups=mesh['dp'=8,'mp'=16] {'mp'}, dimensions={0}, use_global_device_ids=true | all-gather | bytes 2176 | tf_op jit(solution)/shard_map/all_gather | solution.py:441
  310.7 0.6 slice_reduce_fusion
  311.3 0.6 squeeze.10
  311.9 0.6 squeeze.11
  312.5 0.6 squeeze.12
  313.1 0.0 copy-start
  313.1 0.0 all-gather.2.cloned.1.call-done
  313.1 4.1 %bitcast_reduce_fusion = f32[8,8,8192]{2,1,0:T(8,128)} fusion(f32[16,8,8192]{2,1,0:T(8,128)} %all-gather.2.cloned.1.call-done), kind=kLoop, calls=%fused_computation | loop fusion | flops 524288 | bytes 6291456 | tf_op jit(solution)/shard_map/reduce_sum | solution.py:442
  317.2 0.0 copy-done
  317.2 1.3 copy.19
  (1 shorter events, 0.0 us)
Async XLA Ops:
  7.2 262.6 %all-reduce.2.cloned.1.call-start = ((), (), s32[]{:S(2)}) async-start(), calls=%async_computation | async-start | bytes 524288 | tf_op jit(solution)/shard_map/psum | solution.py:439
  182.6 130.4 %all-gather.2.cloned.1.call-start = ((), (), s32[]{:S(2)}) async-start(), calls=%async_computation.1 | async-start | bytes 4456448 | tf_op jit(solution)/shard_map/all_gather | solution.py:440
  313.1 4.1 %copy-start = (bf16[128,8192]{1,0:T(8,128)(2,1)S(1)}, bf16[128,8192]{1,0:T(8,128)(2,1)}, u32[]{:S(2)}) copy-start(bf16[128,8192]{1,0:T(8,128)(2,1)} %get-tuple-element.22) | copy-start | bytes 6291460
Sparse Core Ops, SparseCore 0:
  182.7 86.9 all-reduce.1
  271.6 35.0 all-gather.1

commit v2 on v1

--- a/solution.py
+++ b/solution.py
@@ -16,7 +16,10 @@
 TOTAL = 16384 * QH * HD
 SCALE = HD**-0.5
 KT = 384
-NW = 1536
+NW = 1280
+PIECES = 16
+PIECE = D // PIECES
+PACK = PIECE + L
 FAR = 4
 
 highest = lax.Precision.HIGHEST
@@ -44,11 +47,11 @@
     dtw,
     out,
     gw_out,
-    small_out,
     a_buf,
     w_buf,
     x_send,
     dt_stage,
+    dt_parts,
     acc,
     qb,
     qt,
@@ -57,7 +60,6 @@
     n_buf,
     pb,
     o_buf,
-    pre_t,
     gw,
     small,
     mixed,
@@ -117,7 +119,9 @@
     lax.fori_loop(0, CHUNKS, start_exchange, 0)
 
     w_copies = (
-        pltpu.make_async_copy(dtw, dt_stage, w_sem.at[2]),
+        pltpu.make_async_copy(
+            dtw.at[pl.ds(pl.multiple_of(chip * RATIO, RATIO), RATIO), :], dt_stage, w_sem.at[2]
+        ),
         pltpu.make_async_copy(qw, w_buf.at[:, q_cols], w_sem.at[0]),
         pltpu.make_async_copy(kvw, w_buf.at[:, kv_cols], w_sem.at[1]),
     )
@@ -186,19 +190,11 @@
         c.start()
 
     w_copies[0].wait()
-
-    def split_dt(r, carry):
-        rows = pl.ds(pl.multiple_of(r * 512, 512), 512)
-        w = dt_stage[rows, :]
-        one = w.astype(bf16).astype(f32)
-        left = w - one
-        two = left.astype(bf16).astype(f32)
-        three = left - two
-        w_buf[rows, 1280:1408] = jnp.concatenate([one, two], axis=1).astype(bf16)
-        w_buf[rows, 1408:1536] = jnp.concatenate([three, jnp.zeros_like(three)], axis=1).astype(bf16)
-        return carry
-
-    lax.fori_loop(0, D // 512, split_dt, 0)
+    w = dt_stage[...]
+    one = w.astype(bf16).astype(f32)
+    two = (w - one).astype(bf16).astype(f32)
+    three = w - one - two
+    dt_parts[...] = jnp.concatenate([one, two, three, jnp.zeros_like(w)], axis=0).astype(bf16)
     gw[...] = jnp.zeros_like(gw)
     small[...] = jnp.zeros_like(small)
 
@@ -268,10 +264,10 @@
             pb[rows, :] = weights.astype(bf16)
         o_buf[...] = dot_nn(pb[...], jnp.concatenate([v, jnp.ones_like(v)], axis=1))
 
-        pre = acc[:, 1280:1408] + acc[:, 1408:1536]
-        pre = pre + pltpu.roll(pre, QH, 1)
-        pre_t[...] = pre.T
-        raw = pre_t[pl.ds(pl.multiple_of(chip * RATIO, RATIO), RATIO), :] + per_head(bias_s)
+        pre = dot_nt(dt_parts[:, 0:KB], a_buf[i, 0])
+        for m in range(1, CHIPS):
+            pre += dot_nt(dt_parts[:, m * KB : (m + 1) * KB], a_buf[i, m])
+        raw = pre[0:8] + pre[8:16] + pre[16:24] + per_head(bias_s)
         step_size = jnp.maximum(raw, 0.0) + jnp.log1p(jnp.exp(-jnp.abs(raw)))
         rate = -jnp.exp(per_head(decay_s))
         summed = jnp.dot(step_size, upper, precision=highest, preferred_element_type=f32)
@@ -346,8 +342,14 @@
 
     lax.fori_loop(0, CHUNKS, phase, 0)
 
-    gw_out[...] = gw[0:8, :] + gw[8:16, :]
-    small_out[...] = small[...]
+    packed = jnp.zeros((RATIO, L), f32)
+    for n in range(4):
+        line = jnp.sum(small[n * RATIO : (n + 1) * RATIO, :], axis=1, keepdims=True)
+        packed = jnp.where(col_i[:RATIO] == n, line, packed)
+    for r in range(PIECES):
+        cols = slice(r * PIECE, (r + 1) * PIECE)
+        gw_out[r, :, 0:PIECE] = gw[0:8, cols] + gw[8:16, cols]
+        gw_out[r, :, PIECE:PACK] = packed
 
     def finish(i, carry):
         for kind in range(12):
@@ -374,16 +376,16 @@
         body,
         out_shape=(
             jax.ShapeDtypeStruct((L, D), bf16),
-            jax.ShapeDtypeStruct((RATIO, D), f32),
-            jax.ShapeDtypeStruct((32, L), f32),
+            jax.ShapeDtypeStruct((PIECES, RATIO, PACK), f32),
         ),
         in_specs=[smem, smem, smem, smem, vmem, vmem, hbm, hbm, hbm],
-        out_specs=(hbm, vmem, vmem),
+        out_specs=(hbm, vmem),
         scratch_shapes=[
             pltpu.VMEM((CHUNKS, CHIPS, L, KB), bf16),
             pltpu.VMEM((D, NW), bf16),
             pltpu.VMEM((CHUNKS, L, 512), bf16),
-            pltpu.VMEM((D, QH), f32),
+            pltpu.VMEM((RATIO, D), f32),
+            pltpu.VMEM((32, D), bf16),
             pltpu.VMEM((L, NW), f32),
             pltpu.VMEM(stacked, bf16),
             pltpu.VMEM(stacked, bf16),
@@ -392,7 +394,6 @@
             pltpu.VMEM(stacked, f32),
             pltpu.VMEM(stacked, bf16),
             pltpu.VMEM((RATIO * L, 2 * HD), f32),
-            pltpu.VMEM((L, L), f32),
             pltpu.VMEM((16, D), f32),
             pltpu.VMEM((32, L), f32),
             pltpu.VMEM((CHUNKS, L, KB), bf16),
@@ -413,6 +414,153 @@
     )(order, bias, decay, gain, positions, hidden, qw, kvw, dtw)
 
 
+def reduce_body(
+    mine,
+    grad,
+    rows,
+    loss,
+    got,
+    own,
+    heads,
+    narrow,
+    s1s,
+    s1r,
+    s2s,
+    s2r,
+    s3s,
+    s3r,
+    s4s,
+    s4r,
+):
+    d = lax.axis_index("dp")
+    me = lax.axis_index("mp")
+    core = me % 2
+    chip = me // 2
+    place = d * 2 + core
+
+    def same_chip(step):
+        r = (place + step) % PIECES
+        return {"dp": r // 2, "mp": chip * 2 + r % 2}
+
+    def same_core(step):
+        return {"dp": d, "mp": (chip + step) % CHIPS * 2 + core}
+
+    barrier = pltpu.get_barrier_semaphore()
+    for step in range(1, PIECES):
+        pl.semaphore_signal(barrier, inc=1, device_id=same_chip(step))
+    for step in range(1, CHIPS):
+        pl.semaphore_signal(barrier, inc=1, device_id=same_core(step))
+    pl.semaphore_wait(barrier, PIECES + CHIPS - 2)
+
+    def scatter(step):
+        return pltpu.make_async_remote_copy(
+            src_ref=mine.at[(place + step) % PIECES],
+            dst_ref=got.at[step],
+            send_sem=s1s.at[step],
+            recv_sem=s1r.at[step],
+            device_id=same_chip(step),
+        )
+
+    for step in range(1, PIECES):
+        scatter(step).start()
+    total = mine[place]
+    for step in range(1, PIECES):
+        scatter(step).wait_recv()
+        total += got[step]
+    own[...] = total
+
+    def across_heads(step):
+        return pltpu.make_async_remote_copy(
+            src_ref=own,
+            dst_ref=heads.at[chip],
+            send_sem=s2s.at[step],
+            recv_sem=s2r.at[step],
+            device_id=same_core(step),
+        )
+
+    for step in range(1, CHIPS):
+        across_heads(step).start()
+    heads[chip] = total
+    for step in range(1, CHIPS):
+        across_heads(step).wait_recv()
+    narrow[core, d] = heads[:, :, 0:PIECE].reshape(QH, PIECE).astype(bf16)
+
+    def pieces(step):
+        return pltpu.make_async_remote_copy(
+            src_ref=narrow.at[core, d],
+            dst_ref=narrow.at[core, d],
+            send_sem=s3s.at[step],
+            recv_sem=s3r.at[step],
+            device_id={"dp": (d + step) % 8, "mp": me},
+        )
+
+    def to_partner(step):
+        ref = narrow.at[core, (d + 8 - step) % 8]
+        return pltpu.make_async_remote_copy(
+            src_ref=ref,
+            dst_ref=ref,
+            send_sem=s4s.at[step],
+            recv_sem=s4r.at[step],
+            device_id={"dp": d, "mp": chip * 2 + 1 - core},
+        )
+
+    for step in range(1, 8):
+        pieces(step).start()
+    to_partner(0).start()
+    lines = heads[:, :, PIECE:PACK].reshape(QH, L)
+    lines = jnp.concatenate([lines, jnp.zeros_like(lines)], axis=0).T
+    rows[...] = lines[0:8, :]
+    loss[0, 0] = jnp.sum(lines[3:4, :])
+    for step in range(1, 8):
+        pieces(step).wait_recv()
+        to_partner(step).start()
+    for step in range(8):
+        to_partner(step).wait_recv()
+    for r in range(PIECES):
+        grad[:, r * PIECE : (r + 1) * PIECE] = narrow[r % 2, r // 2].astype(f32)
+    for step in range(1, PIECES):
+        scatter(step).wait_send()
+    for step in range(1, CHIPS):
+        across_heads(step).wait_send()
+    for step in range(1, 8):
+        pieces(step).wait_send()
+    for step in range(8):
+        to_partner(step).wait_send()
+
+
+def reduce_all(mine):
+    vmem = pl.BlockSpec(memory_space=pltpu.VMEM)
+    dma = pltpu.SemaphoreType.DMA
+    return pl.pallas_call(
+        reduce_body,
+        out_shape=(
+            jax.ShapeDtypeStruct((QH, D), f32),
+            jax.ShapeDtypeStruct((8, L), f32),
+            jax.ShapeDtypeStruct((1, 1), f32),
+        ),
+        in_specs=[vmem],
+        out_specs=(vmem, vmem, pl.BlockSpec(memory_space=pltpu.SMEM)),
+        scratch_shapes=[
+            pltpu.VMEM((PIECES, RATIO, PACK), f32),
+            pltpu.VMEM((RATIO, PACK), f32),
+            pltpu.VMEM((CHIPS, RATIO, PACK), f32),
+            pltpu.VMEM((2, 8, QH, PIECE), bf16),
+            dma((PIECES,)),
+            dma((PIECES,)),
+            dma((CHIPS,)),
+            dma((CHIPS,)),
+            dma((8,)),
+            dma((8,)),
+            dma((8,)),
+            dma((8,)),
+        ],
+        name="reduce_all",
+        compiler_params=pltpu.CompilerParams(
+            collective_id=1, has_side_effects=True, vmem_limit_bytes=32 * 2**20
+        ),
+    )(mine)
+
+
 def local(
     hidden_in,
     positions,
@@ -424,7 +572,7 @@
     decay_log,
     skip_gain,
 ):
-    student_out, gw, small = fused(
+    student_out, partial = fused(
         assignment,
         dt_bias,
         decay_log,
@@ -433,15 +581,10 @@
         hidden_in.reshape(16, L, 512),
         query_weight,
         kv_weight,
-        dt_weight,
+        dt_weight.T,
     )
-    sums = jnp.sum(small.reshape(4, RATIO, L), axis=2)
-    gw, sums = lax.psum((gw, sums), "dp")
-    gw = lax.all_gather(gw, "mp", axis=0)
-    sums = lax.all_gather(sums, "mp", axis=0)
-    gw = gw.reshape(CHIPS, 2, RATIO, D).sum(1).reshape(QH, D).T
-    sums = sums.reshape(CHIPS, 2, 4, RATIO).sum(1).transpose(1, 0, 2).reshape(4, QH)
-    return student_out, gw, sums[0], sums[1], sums[2], jnp.sum(sums[3])
+    grad, rows, loss = reduce_all(partial)
+    return student_out, grad.T, rows[0, :QH], rows[1, :QH], rows[2, :QH], loss.reshape(())
 
 
 def solution(mesh):

time: 327 us -> 210 us (0.64)
  waiting for transfers between devices: 87.1 us -> 0 us
  blocking collectives: 39.9 us -> 0 us
  Pallas kernels: 172 us -> 200 us
  between operations: 14.1 us -> 2.41 us
  other arithmetic: 5.6 us -> 0 us
    psum x1 -> x0, waiting for transfers between devices: 87.1 us -> none  [local(): gw, sums = lax.psum((gw, sums), 'dp')]
    pallas_call x0 -> x1, Pallas kernels: none -> 27.9 us  [reduce_all(): pl.pallas_call(reduce_body, out_shape=(jax.ShapeDtypeStruct((QH, D), f32)...]
    psum x1 -> x0, blocking collectives: 20.3 us -> none  [local(): gw, sums = lax.psum((gw, sums), 'dp')]
    all_gather x1 -> x0, blocking collectives: 19.6 us -> none  [local(): sums = lax.all_gather(sums, 'mp', axis=0)]
    reduce_sum x4 -> x0, other arithmetic: 5.6 us -> none  [the longest x1 4.12 us: local(): gw = gw.reshape(CHIPS, 2, RATIO, D).sum(1).reshape(QH, D).T]
  transfers between devices with their start and end apart: 2 -> 0, of which waited for: 1 -> 0; matrix products, arithmetic and copies ran while one was open for 1% -> 0% of each run, Pallas kernels for 0% -> 0%
where the time goes in v2:
time: 210 us; the launch traced here: 208 us
  Pallas kernels  200 us (95%)
  local copies, waits for them, and re-layouts  5.9 us (3%)
  between operations  2.41 us (1%)
    pallas_call x1, Pallas kernels, fused(): pl.pallas_call(body, out_shape=(jax.ShapeDtypeStruct((L, D), bf16), jax.S...  172 us
    pallas_call x1, Pallas kernels, reduce_all(): pl.pallas_call(reduce_body, out_shape=(jax.ShapeDtypeStruct((QH, D), f32)...  27.9 us
    unnamed x4, local copies, waits for them, and re-layouts  5.38 us

profile of v2, /device:TPU:0, one launch (start us, length us, event | category | flops | bytes accessed | tf_op | source)
XLA Modules:
  0.0 207.9 jit_solution(6552210352432521808)
XLA Ops:
  0.6 171.7 %fused.1 = (bf16[128,8192]{1,0:T(8,128)(2,1)}, f32[16,8,640]{2,1,0:T(8,128)}) custom-call(s32[1,16]{1,0:T(1,128)} %order.1, f32[64]{0:T(128)} %bias_s.1, f32[64]{0:T(128)} %decay_s.1, f32[64]{0:T(128)} %gain_s.1, s32[16,128]{1,0:T(8,128)} %bitcast.14, bf16[16,128,512]{2,1,0:T(8,128)(2,1)} %bitcast.12, bf16[8192,512]{1,0:T(8,128)(2,1)} %qw.1, ...), custom_call_target="tpu_custom_call" | custom-call | tf_op jit(solution)/shard_map/fused/pallas_call | solution.py:375
  172.4 0.0 copy-start
  172.4 1.0 copy-done
  173.3 27.9 %reduce_all.1 = (f32[64,8192]{1,0:T(8,128)S(1)}, f32[8,128]{1,0:T(8,128)S(1)}, f32[1,1]{1,0:T(1,128)}) custom-call(f32[16,8,640]{2,1,0:T(8,128)S(1)} %copy-done), custom_call_target="tpu_custom_call" | custom-call | tf_op jit(solution)/shard_map/reduce_all/pallas_call | solution.py:534
  201.2 0.5 slice_bitcast_fusion
  201.8 3.1 %copy.18 = bf16[128,8192]{1,0:T(8,128)(2,1)} copy(bf16[128,8192]{1,0:T(8,128)(2,1)} %get-tuple-element.25) | data formatting | bytes 4194304
  204.9 1.3 copy.19
Async XLA Ops:
  172.4 1.0 copy-start

commit v3 on v1

--- a/solution.py
+++ b/solution.py
@@ -15,9 +15,13 @@
 KB = 1024
 TOTAL = 16384 * QH * HD
 SCALE = HD**-0.5
-KT = 384
-NW = 1536
+KT = 512
+NW = 1280
+PIECES = 16
+PIECE = D // PIECES
+PACK = PIECE + L
 FAR = 4
+SHIFT = 4
 
 highest = lax.Precision.HIGHEST
 f32 = jnp.float32
@@ -43,12 +47,15 @@
     kvw,
     dtw,
     out,
-    gw_out,
-    small_out,
+    narrow,
+    rows_out,
+    loss_out,
+    mine,
     a_buf,
     w_buf,
     x_send,
     dt_stage,
+    dt_parts,
     acc,
     qb,
     qt,
@@ -57,7 +64,6 @@
     n_buf,
     pb,
     o_buf,
-    pre_t,
     gw,
     small,
     mixed,
@@ -70,6 +76,17 @@
     wr_rs,
     o_ss,
     o_rs,
+    got,
+    own,
+    heads,
+    s1s,
+    s1r,
+    s2s,
+    s2r,
+    s3s,
+    s3r,
+    s4s,
+    s4r,
 ):
     me = lax.axis_index("mp")
     core = me % 2
@@ -84,13 +101,30 @@
     def device(xx, yy):
         return (xx * 4 + yy) * 2 + core
 
+    def block(which, i):
+        return which * CHUNKS + (i + SHIFT * which) % CHUNKS
+
+    lag = (y + 2 * x) % 4
+
     partner = chip * 2 + (1 - core)
     to_up, to_down, to_x = device(x, up), device(x, down), device(xo, y)
 
+    d = lax.axis_index("dp")
+    place = d * 2 + core
+
+    def same_chip(step):
+        r = (place + step) % PIECES
+        return {"dp": r // 2, "mp": chip * 2 + r % 2}
+
+    def same_core(step):
+        return {"dp": d, "mp": (chip + step) % CHIPS * 2 + core}
+
     barrier = pltpu.get_barrier_semaphore()
     for step in range(1, 16):
-        pl.semaphore_signal(barrier, inc=1, device_id={"mp": (me + step) % 16})
-    pl.semaphore_wait(barrier, 15)
+        pl.semaphore_signal(barrier, inc=1, device_id={"dp": d, "mp": (me + step) % 16})
+    for step in range(1, PIECES):
+        pl.semaphore_signal(barrier, inc=1, device_id=same_chip(step))
+    pl.semaphore_wait(barrier, 30)
 
     q_cols = pl.ds(pl.multiple_of(core * 512, 512), 512)
     kv_cols = pl.ds(pl.multiple_of(1024 + core * 128, 128), 128)
@@ -101,8 +135,8 @@
         )
 
     def stage(i, carry):
-        a_buf[i, chip, :, q_cols] = x_in[order[0, core * CHUNKS + i]]
-        x_send[i] = x_in[order[0, (1 - core) * CHUNKS + i]]
+        a_buf[i, chip, :, q_cols] = x_in[order[0, block(core, i)]]
+        x_send[i] = x_in[order[0, block(1 - core, i)]]
         return carry
 
     lax.fori_loop(0, CHUNKS, stage, 0)
@@ -117,7 +151,9 @@
     lax.fori_loop(0, CHUNKS, start_exchange, 0)
 
     w_copies = (
-        pltpu.make_async_copy(dtw, dt_stage, w_sem.at[2]),
+        pltpu.make_async_copy(
+            dtw.at[pl.ds(pl.multiple_of(chip * RATIO, RATIO), RATIO), :], dt_stage, w_sem.at[2]
+        ),
         pltpu.make_async_copy(qw, w_buf.at[:, q_cols], w_sem.at[0]),
         pltpu.make_async_copy(kvw, w_buf.at[:, kv_cols], w_sem.at[1]),
     )
@@ -129,8 +165,6 @@
     first = pl.ds(0, KT)
     second = pl.ds(KT, KB - KT)
     every = pl.ds(0, L)
-    low = pl.ds(0, L // 2)
-    high = pl.ds(L // 2, L // 2)
     whole = pl.ds(0, KB)
 
     def hop(kind, i):
@@ -138,10 +172,9 @@
             (x, y, every, whole, to_up),
             (x, y, every, whole, to_down),
             (x, y, every, whole, to_x),
-            (x, down, low, first, to_up),
             (x, down, every, second, to_up),
             (x, down, every, first, to_x),
-            (x, up, high, first, to_down),
+            (x, up, every, first, to_down),
             (x, up, every, first, to_x),
             (xo, y, every, second, to_up),
             (xo, y, every, second, to_down),
@@ -158,24 +191,23 @@
 
     def hop2(i):
         hop(0, i).wait_recv()
-        for kind in (4, 3, 5):
+        for kind in (3, 4):
             hop(kind, i).start()
         hop(1, i).wait_recv()
-        for kind in (6, 7):
+        for kind in (5, 6):
             hop(kind, i).start()
         hop(2, i).wait_recv()
-        for kind in (9, 8):
+        for kind in (8, 7):
             hop(kind, i).start()
 
     def hop3(i):
-        hop(9, i).wait_recv()
-        hop(11, i).start()
-        hop(3, i).wait_recv()
-        hop(6, i).wait_recv()
+        hop(8, i).wait_recv()
         hop(10, i).start()
+        hop(5, i).wait_recv()
+        hop(9, i).start()
 
     def arrived(i):
-        for kind in (4, 5, 7, 8, 10, 11):
+        for kind in (3, 4, 6, 7, 9, 10):
             hop(kind, i).wait_recv()
 
     for i in range(FAR):
@@ -186,19 +218,11 @@
         c.start()
 
     w_copies[0].wait()
-
-    def split_dt(r, carry):
-        rows = pl.ds(pl.multiple_of(r * 512, 512), 512)
-        w = dt_stage[rows, :]
-        one = w.astype(bf16).astype(f32)
-        left = w - one
-        two = left.astype(bf16).astype(f32)
-        three = left - two
-        w_buf[rows, 1280:1408] = jnp.concatenate([one, two], axis=1).astype(bf16)
-        w_buf[rows, 1408:1536] = jnp.concatenate([three, jnp.zeros_like(three)], axis=1).astype(bf16)
-        return carry
-
-    lax.fori_loop(0, D // 512, split_dt, 0)
+    w = dt_stage[...]
+    one = w.astype(bf16).astype(f32)
+    two = (w - one).astype(bf16).astype(f32)
+    three = w - one - two
+    dt_parts[...] = jnp.concatenate([one, two, three, jnp.zeros_like(w)], axis=0).astype(bf16)
     gw[...] = jnp.zeros_like(gw)
     small[...] = jnp.zeros_like(small)
 
@@ -217,7 +241,7 @@
 
     def out_copy(i):
         dst = out.at[:, pl.ds(pl.multiple_of(chip * KB, KB), KB)]
-        target = core * CHUNKS + i
+        target = block(core, i)
 
         def far():
             return remote(mixed.at[i], dst, o_ss.at[i], o_rs.at[chip], target)
@@ -226,6 +250,11 @@
             return pltpu.make_async_copy(mixed.at[i], dst, o_rs.at[chip])
 
         return target, far, near
+
+    def send_out(i):
+        target, far, near = out_copy(i)
+        pl.when(target == me)(lambda: near().start())
+        pl.when(target != me)(lambda: far().start())
 
     def compute(i):
         def project(n, carry):
@@ -238,7 +267,7 @@
 
         lax.fori_loop(0, NW // 256, project, 0)
 
-        spots = positions[pl.ds(order[0, core * CHUNKS + i], 1), :].astype(f32)
+        spots = positions[pl.ds(order[0, block(core, i)], 1), :].astype(f32)
         spots = jnp.broadcast_to(spots, (L, L)).T
         lane = col_i % (HD // 2)
         frequency = jnp.exp(lane.astype(f32) * f32(-2.0 / HD * 13.122363377404328))
@@ -268,10 +297,10 @@
             pb[rows, :] = weights.astype(bf16)
         o_buf[...] = dot_nn(pb[...], jnp.concatenate([v, jnp.ones_like(v)], axis=1))
 
-        pre = acc[:, 1280:1408] + acc[:, 1408:1536]
-        pre = pre + pltpu.roll(pre, QH, 1)
-        pre_t[...] = pre.T
-        raw = pre_t[pl.ds(pl.multiple_of(chip * RATIO, RATIO), RATIO), :] + per_head(bias_s)
+        pre = dot_nt(dt_parts[:, 0:KB], a_buf[i, 0])
+        for m in range(1, CHIPS):
+            pre += dot_nt(dt_parts[:, m * KB : (m + 1) * KB], a_buf[i, m])
+        raw = pre[0:8] + pre[8:16] + pre[16:24] + per_head(bias_s)
         step_size = jnp.maximum(raw, 0.0) + jnp.log1p(jnp.exp(-jnp.abs(raw)))
         rate = -jnp.exp(per_head(decay_s))
         summed = jnp.dot(step_size, upper, precision=highest, preferred_element_type=f32)
@@ -295,9 +324,10 @@
             gain_rows.append(jnp.sum(differ * v32, axis=0, keepdims=True))
             loss_rows.append(jnp.sum(differ * differ, axis=0, keepdims=True))
             pb[rows, :] = differ.astype(bf16)
-        target, far, near = out_copy(i)
-        pl.when(target == me)(lambda: near().start())
-        pl.when(target != me)(lambda: far().start())
+
+        @pl.when(i >= lag)
+        def _():
+            send_out(i - lag)
 
         s_t[...] = dot_nt(pb[...], v)
         col_rows, row_cols = [], jnp.zeros((L, L), f32)
@@ -324,6 +354,77 @@
             cols = slice(m * KB, (m + 1) * KB)
             gw[:, cols] += dot_nn(parts, a_buf[i, m])
 
+    def scatter(step):
+        return pltpu.make_async_remote_copy(
+            src_ref=mine.at[(place + step) % PIECES],
+            dst_ref=got.at[step],
+            send_sem=s1s.at[step],
+            recv_sem=s1r.at[step],
+            device_id=same_chip(step),
+        )
+
+    def across_heads(step):
+        return pltpu.make_async_remote_copy(
+            src_ref=own,
+            dst_ref=heads.at[chip],
+            send_sem=s2s.at[step],
+            recv_sem=s2r.at[step],
+            device_id=same_core(step),
+        )
+
+    def columns(dd):
+        at = (dd * 2 + core) * PIECE
+        return narrow.at[:, pl.ds(pl.multiple_of(at, PIECE), PIECE)]
+
+    def pieces(step):
+        return pltpu.make_async_remote_copy(
+            src_ref=columns(d),
+            dst_ref=columns(d),
+            send_sem=s3s.at[step],
+            recv_sem=s3r.at[step],
+            device_id={"dp": (d + step) % 8, "mp": me},
+        )
+
+    def to_partner(step):
+        ref = columns((d + 8 - step) % 8)
+        return remote(ref, ref, s4s.at[step], s4r.at[step], partner)
+
+    def sum_up():
+        for step in range(1, PIECES):
+            scatter(step).start()
+        total = mine[place]
+        for step in range(1, PIECES):
+            scatter(step).wait_recv()
+            total += got[step]
+        own[...] = total
+        for step in range(1, CHIPS):
+            across_heads(step).start()
+        heads[chip] = total
+        for step in range(1, CHIPS):
+            across_heads(step).wait_recv()
+        at = pl.multiple_of(place * PIECE, PIECE)
+        narrow[:, pl.ds(at, PIECE)] = heads[:, :, 0:PIECE].reshape(QH, PIECE).astype(bf16)
+        for step in range(1, 8):
+            pieces(step).start()
+        to_partner(0).start()
+        lines = heads[:, :, PIECE:PACK].reshape(QH, L)
+        lines = jnp.concatenate([lines, jnp.zeros_like(lines)], axis=0).T
+        rows_out[...] = lines[0:8, :]
+        loss_out[0, 0] = jnp.sum(lines[3:4, :])
+        for step in range(1, 8):
+            pieces(step).wait_recv()
+            to_partner(step).start()
+        for step in range(8):
+            to_partner(step).wait_recv()
+        for step in range(1, PIECES):
+            scatter(step).wait_send()
+        for step in range(1, CHIPS):
+            across_heads(step).wait_send()
+        for step in range(1, 8):
+            pieces(step).wait_send()
+        for step in range(8):
+            to_partner(step).wait_send()
+
     hop2(0)
     hop2(1)
     hop3(0)
@@ -346,11 +447,23 @@
 
     lax.fori_loop(0, CHUNKS, phase, 0)
 
-    gw_out[...] = gw[0:8, :] + gw[8:16, :]
-    small_out[...] = small[...]
+    def send_late(i, carry):
+        pl.when(i + lag >= CHUNKS)(lambda: send_out(i))
+        return carry
+
+    lax.fori_loop(0, CHUNKS, send_late, 0)
+    packed = jnp.zeros((RATIO, L), f32)
+    for n in range(4):
+        line = jnp.sum(small[n * RATIO : (n + 1) * RATIO, :], axis=1, keepdims=True)
+        packed = jnp.where(col_i[:RATIO] == n, line, packed)
+    for r in range(PIECES):
+        cols = slice(r * PIECE, (r + 1) * PIECE)
+        mine[r, :, 0:PIECE] = gw[0:8, cols] + gw[8:16, cols]
+        mine[r, :, PIECE:PACK] = packed
+    sum_up()
 
     def finish(i, carry):
-        for kind in range(12):
+        for kind in range(11):
             hop(kind, i).wait_send()
         exchange(i).wait_send()
         target, far, _ = out_copy(i)
@@ -374,16 +487,19 @@
         body,
         out_shape=(
             jax.ShapeDtypeStruct((L, D), bf16),
-            jax.ShapeDtypeStruct((RATIO, D), f32),
-            jax.ShapeDtypeStruct((32, L), f32),
+            jax.ShapeDtypeStruct((QH, D), bf16),
+            jax.ShapeDtypeStruct((8, L), f32),
+            jax.ShapeDtypeStruct((1, 1), f32),
         ),
         in_specs=[smem, smem, smem, smem, vmem, vmem, hbm, hbm, hbm],
-        out_specs=(hbm, vmem, vmem),
+        out_specs=(hbm, vmem, vmem, smem),
         scratch_shapes=[
+            pltpu.VMEM((PIECES, RATIO, PACK), f32),
             pltpu.VMEM((CHUNKS, CHIPS, L, KB), bf16),
             pltpu.VMEM((D, NW), bf16),
             pltpu.VMEM((CHUNKS, L, 512), bf16),
-            pltpu.VMEM((D, QH), f32),
+            pltpu.VMEM((RATIO, D), f32),
+            pltpu.VMEM((32, D), bf16),
             pltpu.VMEM((L, NW), f32),
             pltpu.VMEM(stacked, bf16),
             pltpu.VMEM(stacked, bf16),
@@ -392,19 +508,29 @@
             pltpu.VMEM(stacked, f32),
             pltpu.VMEM(stacked, bf16),
             pltpu.VMEM((RATIO * L, 2 * HD), f32),
-            pltpu.VMEM((L, L), f32),
             pltpu.VMEM((16, D), f32),
             pltpu.VMEM((32, L), f32),
             pltpu.VMEM((CHUNKS, L, KB), bf16),
             dma((CHUNKS,)),
             dma((CHUNKS,)),
-            dma((CHUNKS, 12)),
-            dma((CHUNKS, 12)),
+            dma((CHUNKS, 11)),
+            dma((CHUNKS, 11)),
             dma((3,)),
             dma((2,)),
             dma((2,)),
             dma((CHUNKS,)),
             dma((CHIPS,)),
+            pltpu.VMEM((PIECES, RATIO, PACK), f32),
+            pltpu.VMEM((RATIO, PACK), f32),
+            pltpu.VMEM((CHIPS, RATIO, PACK), f32),
+            dma((PIECES,)),
+            dma((PIECES,)),
+            dma((CHIPS,)),
+            dma((CHIPS,)),
+            dma((8,)),
+            dma((8,)),
+            dma((8,)),
+            dma((8,)),
         ],
         name="fused",
         compiler_params=pltpu.CompilerParams(
@@ -424,7 +550,7 @@
     decay_log,
     skip_gain,
 ):
-    student_out, gw, small = fused(
+    student_out, narrow, rows, loss = fused(
         assignment,
         dt_bias,
         decay_log,
@@ -433,15 +559,10 @@
         hidden_in.reshape(16, L, 512),
         query_weight,
         kv_weight,
-        dt_weight,
+        dt_weight.T,
     )
-    sums = jnp.sum(small.reshape(4, RATIO, L), axis=2)
-    gw, sums = lax.psum((gw, sums), "dp")
-    gw = lax.all_gather(gw, "mp", axis=0)
-    sums = lax.all_gather(sums, "mp", axis=0)
-    gw = gw.reshape(CHIPS, 2, RATIO, D).sum(1).reshape(QH, D).T
-    sums = sums.reshape(CHIPS, 2, 4, RATIO).sum(1).transpose(1, 0, 2).reshape(4, QH)
-    return student_out, gw, sums[0], sums[1], sums[2], jnp.sum(sums[3])
+    grad = narrow.astype(f32)
+    return student_out, grad.T, rows[0, :QH], rows[1, :QH], rows[2, :QH], loss.reshape(())
 
 
 def solution(mesh):

time: 327 us -> 194 us (0.59)
  waiting for transfers between devices: 87.1 us -> 0 us
  blocking collectives: 39.9 us -> 0 us
  Pallas kernels: 172 us -> 185 us
  between operations: 14.1 us -> 2.33 us
  local copies, waits for them, and re-layouts: 6.95 us -> 2.68 us
    psum x1 -> x0, waiting for transfers between devices: 87.1 us -> none  [local(): gw, sums = lax.psum((gw, sums), 'dp')]
    psum x1 -> x0, blocking collectives: 20.3 us -> none  [local(): gw, sums = lax.psum((gw, sums), 'dp')]
    all_gather x1 -> x0, blocking collectives: 19.6 us -> none  [local(): sums = lax.all_gather(sums, 'mp', axis=0)]
    pallas_call x1, Pallas kernels: 172 us -> 185 us  [fused(): pl.pallas_call(body, out_shape=(jax.ShapeDtypeStruct((L, D), bf16), jax.S...]
    reduce_sum x4 -> x0, other arithmetic: 5.6 us -> none  [the longest x1 4.12 us: local(): gw = gw.reshape(CHIPS, 2, RATIO, D).sum(1).reshape(QH, D).T]
    unnamed x4 -> x3, local copies, waits for them, and re-layouts: 5.09 us -> 1.32 us
  transfers between devices with their start and end apart: 2 -> 0, of which waited for: 1 -> 0; matrix products, arithmetic and copies ran while one was open for 1% -> 0% of each run, Pallas kernels for 0% -> 0%
where the time goes in v3:
time: 194 us; the launch traced here: 193 us
  Pallas kernels  185 us (95%)
  local copies, waits for them, and re-layouts  2.68 us (1%)
  other arithmetic  2.68 us (1%)
  between operations  2.33 us (1%)
    pallas_call x1, Pallas kernels, fused(): pl.pallas_call(body, out_shape=(jax.ShapeDtypeStruct((L, D), bf16), jax.S...  185 us

profile of v3, /device:TPU:0, one launch (start us, length us, event | category | flops | bytes accessed | tf_op | source)
XLA Modules:
  0.0 192.9 jit_solution(9079505109742558423)
XLA Ops:
  0.6 185.2 %fused.1 = (bf16[128,8192]{1,0:T(8,128)(2,1)}, bf16[64,8192]{1,0:T(8,128)(2,1)}, f32[8,128]{1,0:T(8,128)}, f32[1,1]{1,0:T(1,128)}) custom-call(s32[1,16]{1,0:T(1,128)} %order.1, f32[64]{0:T(128)} %bias_s.1, f32[64]{0:T(128)} %decay_s.1, f32[64]{0:T(128)} %gain_s.1, s32[16,128]{1,0:T(8,128)} %bitcast.14, bf16[16,128,512]{2,1,0:T(8,128)(2,1)} %bitcast.12, ...), custom_call_target="tpu_custom_call" | custom-call | tf_op jit(solution)/shard_map/fused/pallas_call | solution.py:486
  185.9 0.0 copy-start
  185.9 1.4 slice_bitcast_fusion
  187.2 2.7 %convert_bitcast_fusion = f32[8192,64]{0,1:T(8,128)} fusion(bf16[64,8192]{1,0:T(8,128)(2,1)} %get-tuple-element.11), kind=kLoop, calls=%fused_computation | loop fusion | flops 524288 | bytes 3145728 | tf_op jit(solution)/shard_map/transpose | solution.py:565
  189.9 0.0 copy-done
  189.9 1.3 copy.17
Async XLA Ops:
  185.9 4.1 %copy-start = (bf16[128,8192]{1,0:T(8,128)(2,1)S(1)}, bf16[128,8192]{1,0:T(8,128)(2,1)}, u32[]{:S(2)}) copy-start(bf16[128,8192]{1,0:T(8,128)(2,1)} %get-tuple-element.23) | copy-start | bytes 6291460

commit v4 on v3

--- a/solution.py
+++ b/solution.py
@@ -15,12 +15,15 @@
 KB = 1024
 TOTAL = 16384 * QH * HD
 SCALE = HD**-0.5
-KT = 512
+KT = (384, 512)
 NW = 1280
 PIECES = 16
 PIECE = D // PIECES
 PACK = PIECE + L
 FAR = 4
+EARLY = 2
+FIRST = 2
+SECOND = 4
 SHIFT = 4
 
 highest = lax.Precision.HIGHEST
@@ -104,8 +107,6 @@
     def block(which, i):
         return which * CHUNKS + (i + SHIFT * which) % CHUNKS
 
-    lag = (y + 2 * x) % 4
-
     partner = chip * 2 + (1 - core)
     to_up, to_down, to_x = device(x, up), device(x, down), device(xo, y)
 
@@ -162,56 +163,69 @@
         remote(kvw, w_buf.at[:, kv_cols], wr_ss.at[1], wr_rs.at[1], partner),
     )
 
-    first = pl.ds(0, KT)
-    second = pl.ds(KT, KB - KT)
     every = pl.ds(0, L)
     whole = pl.ds(0, KB)
 
-    def hop(kind, i):
+    low = pl.ds(0, L // 2)
+    high = pl.ds(L // 2, L // 2)
+
+    def hop(kind, i, kt):
+        first = pl.ds(0, kt)
+        second = pl.ds(kt, KB - kt)
         slot_x, slot_y, rows, cols, dev = (
             (x, y, every, whole, to_up),
             (x, y, every, whole, to_down),
             (x, y, every, whole, to_x),
             (x, down, every, second, to_up),
             (x, down, every, first, to_x),
-            (x, up, every, first, to_down),
+            (x, up, high, first, to_down),
             (x, up, every, first, to_x),
             (xo, y, every, second, to_up),
             (xo, y, every, second, to_down),
             (x, across, every, first, to_x),
             (xo, up, every, second, to_down),
+            (x, down, low, first, to_up),
         )[kind]
         ref = a_buf.at[i, slot_x * 4 + slot_y, rows, cols]
         return remote(ref, ref, g_ss.at[i, kind], g_rs.at[i, kind], dev)
 
-    def hop1(i):
+    def hop1(i, kt):
         exchange(i).wait_recv()
         for kind in (0, 1, 2):
-            hop(kind, i).start()
-
-    def hop2(i):
-        hop(0, i).wait_recv()
-        for kind in (3, 4):
-            hop(kind, i).start()
-        hop(1, i).wait_recv()
+            hop(kind, i, kt).start()
+
+    def hop2(i, kt):
+        hop(0, i, kt).wait_recv()
+        for kind in (3, 11, 4):
+            hop(kind, i, kt).start()
+        hop(1, i, kt).wait_recv()
         for kind in (5, 6):
-            hop(kind, i).start()
-        hop(2, i).wait_recv()
+            hop(kind, i, kt).start()
+        hop(2, i, kt).wait_recv()
         for kind in (8, 7):
-            hop(kind, i).start()
-
-    def hop3(i):
-        hop(8, i).wait_recv()
-        hop(10, i).start()
-        hop(5, i).wait_recv()
-        hop(9, i).start()
-
-    def arrived(i):
+            hop(kind, i, kt).start()
+
+    def hop3(i, kt):
+        hop(8, i, kt).wait_recv()
+        hop(10, i, kt).start()
+        hop(5, i, kt).wait_recv()
+        hop(11, i, kt).wait_recv()
+        hop(9, i, kt).start()
+
+    def arrived(i, kt):
         for kind in (3, 4, 6, 7, 9, 10):
-            hop(kind, i).wait_recv()
+            hop(kind, i, kt).wait_recv()
+
+    def all_sent(i, kt):
+        for kind in range(12):
+            hop(kind, i, kt).wait_send()
+
+    def in_turn(step, i):
+        for odd in range(2):
+            pl.when((i < CHUNKS) & (i % 2 == odd))(lambda: step(i, KT[odd]))
 
     for i in range(FAR):
-        hop1(i)
+        hop1(i, KT[i % 2])
     for c in w_copies:
         c.start()
     for c in w_remote:
@@ -325,9 +339,9 @@
             loss_rows.append(jnp.sum(differ * differ, axis=0, keepdims=True))
             pb[rows, :] = differ.astype(bf16)
 
-        @pl.when(i >= lag)
+        @pl.when(i >= CHUNKS - EARLY)
         def _():
-            send_out(i - lag)
+            send_out((chip + i) % EARLY)
 
         s_t[...] = dot_nt(pb[...], v)
         col_rows, row_cols = [], jnp.zeros((L, L), f32)
@@ -389,9 +403,17 @@
         ref = columns((d + 8 - step) % 8)
         return remote(ref, ref, s4s.at[step], s4r.at[step], partner)
 
+    def send_rest(begin, end):
+        def send(i, carry):
+            send_out(EARLY + (chip + i) % (CHUNKS - EARLY))
+            return carry
+
+        lax.fori_loop(begin, end, send, 0)
+
     def sum_up():
         for step in range(1, PIECES):
             scatter(step).start()
+        send_rest(0, FIRST)
         total = mine[place]
         for step in range(1, PIECES):
             scatter(step).wait_recv()
@@ -399,6 +421,7 @@
         own[...] = total
         for step in range(1, CHIPS):
             across_heads(step).start()
+        send_rest(FIRST, SECOND)
         heads[chip] = total
         for step in range(1, CHIPS):
             across_heads(step).wait_recv()
@@ -407,6 +430,7 @@
         for step in range(1, 8):
             pieces(step).start()
         to_partner(0).start()
+        send_rest(SECOND, CHUNKS - EARLY)
         lines = heads[:, :, PIECE:PACK].reshape(QH, L)
         lines = jnp.concatenate([lines, jnp.zeros_like(lines)], axis=0).T
         rows_out[...] = lines[0:8, :]
@@ -425,14 +449,14 @@
         for step in range(8):
             to_partner(step).wait_send()
 
-    hop2(0)
-    hop2(1)
-    hop3(0)
+    hop2(0, KT[0])
+    hop2(1, KT[1])
+    hop3(0, KT[0])
 
     def phase(i, carry):
-        pl.when(i + 1 < CHUNKS)(lambda: hop3(i + 1))
-        pl.when(i + 2 < CHUNKS)(lambda: hop2(i + 2))
-        pl.when(i + FAR < CHUNKS)(lambda: hop1(i + FAR))
+        in_turn(hop3, i + 1)
+        in_turn(hop2, i + 2)
+        in_turn(hop1, i + FAR)
 
         @pl.when(i == 0)
         def _():
@@ -441,17 +465,12 @@
             for c in w_remote:
                 c.wait_recv()
 
-        arrived(i)
+        in_turn(arrived, i)
         compute(i)
         return carry
 
     lax.fori_loop(0, CHUNKS, phase, 0)
 
-    def send_late(i, carry):
-        pl.when(i + lag >= CHUNKS)(lambda: send_out(i))
-        return carry
-
-    lax.fori_loop(0, CHUNKS, send_late, 0)
     packed = jnp.zeros((RATIO, L), f32)
     for n in range(4):
         line = jnp.sum(small[n * RATIO : (n + 1) * RATIO, :], axis=1, keepdims=True)
@@ -463,8 +482,7 @@
     sum_up()
 
     def finish(i, carry):
-        for kind in range(11):
-            hop(kind, i).wait_send()
+        in_turn(all_sent, i)
         exchange(i).wait_send()
         target, far, _ = out_copy(i)
         pl.when(target != me)(lambda: far().wait_send())
@@ -513,8 +531,8 @@
             pltpu.VMEM((CHUNKS, L, KB), bf16),
             dma((CHUNKS,)),
             dma((CHUNKS,)),
-            dma((CHUNKS, 11)),
-            dma((CHUNKS, 11)),
+            dma((CHUNKS, 12)),
+            dma((CHUNKS, 12)),
             dma((3,)),
             dma((2,)),
             dma((2,)),

time: 194 us -> 179 us (0.923)
  the two profiles are of different devices: /device:TPU:0 before, /device:TPU:17 now
where the time goes in v4:
time: 179 us
  Pallas kernels  171 us (96%)
  local copies, waits for them, and re-layouts  2.68 us (1%)
  other arithmetic  2.68 us (1%)
  between operations  2.33 us (1%)
    pallas_call x1, Pallas kernels, fused(): pl.pallas_call(body, out_shape=(jax.ShapeDtypeStruct((L, D), bf16), jax.S...  171 us

profile of v4, /device:TPU:17, one launch (start us, length us, event | category | flops | bytes accessed | tf_op | source)
XLA Modules:
  0.0 178.9 jit_solution(17122126992117294703)
XLA Ops:
  0.6 171.2 %fused.1 = (bf16[128,8192]{1,0:T(8,128)(2,1)}, bf16[64,8192]{1,0:T(8,128)(2,1)}, f32[8,128]{1,0:T(8,128)}, f32[1,1]{1,0:T(1,128)}) custom-call(s32[1,16]{1,0:T(1,128)} %order.1, f32[64]{0:T(128)} %bias_s.1, f32[64]{0:T(128)} %decay_s.1, f32[64]{0:T(128)} %gain_s.1, s32[16,128]{1,0:T(8,128)} %bitcast.14, bf16[16,128,512]{2,1,0:T(8,128)(2,1)} %bitcast.12, ...), custom_call_target="tpu_custom_call" | custom-call | tf_op jit(solution)/shard_map/fused/pallas_call | solution.py:504
  171.9 0.0 copy-start
  171.9 1.4 slice_bitcast_fusion
  173.2 2.7 %convert_bitcast_fusion = f32[8192,64]{0,1:T(8,128)} fusion(bf16[64,8192]{1,0:T(8,128)(2,1)} %get-tuple-element.11), kind=kLoop, calls=%fused_computation | loop fusion | flops 524288 | bytes 3145728 | tf_op jit(solution)/shard_map/transpose | solution.py:583
  175.9 0.0 copy-done
  175.9 1.3 copy.17
Async XLA Ops:
  171.9 4.1 %copy-start = (bf16[128,8192]{1,0:T(8,128)(2,1)S(1)}, bf16[128,8192]{1,0:T(8,128)(2,1)}, u32[]{:S(2)}) copy-start(bf16[128,8192]{1,0:T(8,128)(2,1)} %get-tuple-element.23) | copy-start | bytes 6291460

commit v5 on v4

--- a/solution.py
+++ b/solution.py
@@ -21,9 +21,9 @@
 PIECE = D // PIECES
 PACK = PIECE + L
 FAR = 4
-EARLY = 2
-FIRST = 2
-SECOND = 4
+EARLY = 4
+FIRST = 1
+SECOND = 2
 SHIFT = 4
 
 highest = lax.Precision.HIGHEST
@@ -105,7 +105,7 @@
         return (xx * 4 + yy) * 2 + core
 
     def block(which, i):
-        return which * CHUNKS + (i + SHIFT * which) % CHUNKS
+        return which * CHUNKS + (2 * i + 1 - which + (2 * which - 1) * (i // 4)) % CHUNKS
 
     partner = chip * 2 + (1 - core)
     to_up, to_down, to_x = device(x, up), device(x, down), device(xo, y)
@@ -338,10 +338,6 @@
             gain_rows.append(jnp.sum(differ * v32, axis=0, keepdims=True))
             loss_rows.append(jnp.sum(differ * differ, axis=0, keepdims=True))
             pb[rows, :] = differ.astype(bf16)
-
-        @pl.when(i >= CHUNKS - EARLY)
-        def _():
-            send_out((chip + i) % EARLY)
 
         s_t[...] = dot_nt(pb[...], v)
         col_rows, row_cols = [], jnp.zeros((L, L), f32)
@@ -466,6 +462,12 @@
                 c.wait_recv()
 
         in_turn(arrived, i)
+
+        @pl.when(i >= CHUNKS - EARLY // 2)
+        def _():
+            for n in range(2):
+                send_out((i - (CHUNKS - EARLY // 2)) * 2 + (chip + n) % 2)
+
         compute(i)
         return carry
 

time: 179 us -> 174 us (0.972)
  the two profiles are of different devices: /device:TPU:17 before, /device:TPU:0 now
where the time goes in v5:
time: 174 us
  Pallas kernels  166 us (95%)
  local copies, waits for them, and re-layouts  2.68 us (2%)
  other arithmetic  2.68 us (2%)
  between operations  2.33 us (1%)
    pallas_call x1, Pallas kernels, fused(): pl.pallas_call(body, out_shape=(jax.ShapeDtypeStruct((L, D), bf16), jax.S...  166 us

profile of v5, /device:TPU:0, one launch (start us, length us, event | category | flops | bytes accessed | tf_op | source)
XLA Modules:
  0.0 174.0 jit_solution(14837728759930290707)
XLA Ops:
  0.6 166.3 %fused.1 = (bf16[128,8192]{1,0:T(8,128)(2,1)}, bf16[64,8192]{1,0:T(8,128)(2,1)}, f32[8,128]{1,0:T(8,128)}, f32[1,1]{1,0:T(1,128)}) custom-call(s32[1,16]{1,0:T(1,128)} %order.1, f32[64]{0:T(128)} %bias_s.1, f32[64]{0:T(128)} %decay_s.1, f32[64]{0:T(128)} %gain_s.1, s32[16,128]{1,0:T(8,128)} %bitcast.14, bf16[16,128,512]{2,1,0:T(8,128)(2,1)} %bitcast.12, ...), custom_call_target="tpu_custom_call" | custom-call | tf_op jit(solution)/shard_map/fused/pallas_call | solution.py:506
  166.9 0.0 copy-start
  166.9 1.4 slice_bitcast_fusion
  168.3 2.7 %convert_bitcast_fusion = f32[8192,64]{0,1:T(8,128)} fusion(bf16[64,8192]{1,0:T(8,128)(2,1)} %get-tuple-element.11), kind=kLoop, calls=%fused_computation | loop fusion | flops 524288 | bytes 3145728 | tf_op jit(solution)/shard_map/transpose | solution.py:585
  171.0 0.0 copy-done
  171.0 1.3 copy.17
Async XLA Ops:
  166.9 4.1 %copy-start = (bf16[128,8192]{1,0:T(8,128)(2,1)S(1)}, bf16[128,8192]{1,0:T(8,128)(2,1)}, u32[]{:S(2)}) copy-start(bf16[128,8192]{1,0:T(8,128)(2,1)} %get-tuple-element.23) | copy-start | bytes 6291460

commit v6 on v5

--- a/solution.py
+++ b/solution.py
@@ -135,21 +135,16 @@
             src_ref=src, dst_ref=dst, send_sem=ss, recv_sem=rs, device_id={"mp": dev}
         )
 
-    def stage(i, carry):
-        a_buf[i, chip, :, q_cols] = x_in[order[0, block(core, i)]]
-        x_send[i] = x_in[order[0, block(1 - core, i)]]
-        return carry
-
-    lax.fori_loop(0, CHUNKS, stage, 0)
-
     def exchange(i):
         return remote(x_send.at[i], a_buf.at[i, chip, :, q_cols], ex_ss.at[i], ex_rs.at[i], partner)
 
-    def start_exchange(i, carry):
+    def stage(i, carry):
+        x_send[i] = x_in[order[0, block(1 - core, i)]]
         exchange(i).start()
+        a_buf[i, chip, :, q_cols] = x_in[order[0, block(core, i)]]
         return carry
 
-    lax.fori_loop(0, CHUNKS, start_exchange, 0)
+    lax.fori_loop(0, FAR, stage, 0)
 
     w_copies = (
         pltpu.make_async_copy(
@@ -226,6 +221,7 @@
 
     for i in range(FAR):
         hop1(i, KT[i % 2])
+    lax.fori_loop(FAR, CHUNKS, stage, 0)
     for c in w_copies:
         c.start()
     for c in w_remote:

time: 174 us -> 174 us (level)
  no operation moved by 1% of the time
where the time goes in v6:
time: 174 us
  Pallas kernels  166 us (95%)
  local copies, waits for them, and re-layouts  2.68 us (2%)
  other arithmetic  2.68 us (2%)
  between operations  2.33 us (1%)
    pallas_call x1, Pallas kernels, fused(): pl.pallas_call(body, out_shape=(jax.ShapeDtypeStruct((L, D), bf16), jax.S...  166 us

profile of v6, /device:TPU:0, one launch (start us, length us, event | category | flops | bytes accessed | tf_op | source)
XLA Modules:
  0.0 173.7 jit_solution(8391677970660376730)
XLA Ops:
  0.6 166.0 %fused.1 = (bf16[128,8192]{1,0:T(8,128)(2,1)}, bf16[64,8192]{1,0:T(8,128)(2,1)}, f32[8,128]{1,0:T(8,128)}, f32[1,1]{1,0:T(1,128)}) custom-call(s32[1,16]{1,0:T(1,128)} %order.1, f32[64]{0:T(128)} %bias_s.1, f32[64]{0:T(128)} %decay_s.1, f32[64]{0:T(128)} %gain_s.1, s32[16,128]{1,0:T(8,128)} %bitcast.14, bf16[16,128,512]{2,1,0:T(8,128)(2,1)} %bitcast.12, ...), custom_call_target="tpu_custom_call" | custom-call | tf_op jit(solution)/shard_map/fused/pallas_call | solution.py:502
  166.7 0.0 copy-start
  166.7 1.4 slice_bitcast_fusion
  168.0 2.7 %convert_bitcast_fusion = f32[8192,64]{0,1:T(8,128)} fusion(bf16[64,8192]{1,0:T(8,128)(2,1)} %get-tuple-element.11), kind=kLoop, calls=%fused_computation | loop fusion | flops 524288 | bytes 3145728 | tf_op jit(solution)/shard_map/transpose | solution.py:581
  170.7 0.0 copy-done
  170.7 1.3 copy.17
Async XLA Ops:
  166.7 4.1 %copy-start = (bf16[128,8192]{1,0:T(8,128)(2,1)S(1)}, bf16[128,8192]{1,0:T(8,128)(2,1)}, u32[]{:S(2)}) copy-start(bf16[128,8192]{1,0:T(8,128)(2,1)} %get-tuple-element.23) | copy-start | bytes 6291460
